TPU v7x, 256 devices: a whole 4x4x8 slice. The times are simulated.
256 devices in a mesh: lon: 16 (over y, x_lo, core), lat: 16 (over x_hi, z).
Axes of the slice: x: 4 (x_hi: 2, x_lo: 2; x = x_hi * 2 + x_lo), y: 4, z: 8, core: 2. Of those that a mesh axis runs over, the one named last changes fastest.
Arguments:
- latent: float32 [128, 1024, 128], P('lat', 'lon'), may hold values from -6 to 6
- conv1_weight: float32 [3, 3, 128, 256], replicated, may hold values from -0.1875 to 0.1875
- conv1_bias: float32 [256], replicated, may hold values from -3 to 3
- conv2_weight: float32 [3, 3, 256, 256], replicated, may hold values from -0.125 to 0.125
- conv2_bias: float32 [256], replicated, may hold values from -3 to 3
- head_weight: float32 [256, 4416], replicated, may hold values from -0.375 to 0.375
- head_bias: float32 [4416], replicated, may hold values from -3 to 3
- land_sea: int32 [1024, 8192], P('lat', 'lon'), may hold values 0 or 1
- var_ok: int32 [2, 69], replicated, may hold values 0 or 1
- obs_error: float32 [69], replicated, may hold values from 1 to 3
- obs_band: int32 [16, 1536, 1], P('lon'), may hold values from 0 to 15; in each aligned block of 96 rows (0 to 95, 96 to 191, ..., all dimensions but the last counted through in order) at most 12 rows name the same one
- obs_cell: int32 [16, 1536], P('lon'), may hold values from 0 to 511
- obs_count: int32 [16, 1536], P('lon'), may hold values from 0 to 8
- obs_value: float32 [16, 1536, 4416], P('lon', 'lat'), may hold values from -6 to 6
Outputs:
- grad_latent: float32 [128, 1024, 128], P('lat', 'lon')
Inputs may be any that keep to these rules, and one draw needn't show every extreme that they name: `obs_band`: among the 96 slots of one device (aligned blocks of a sector's list) no band is named more than 12 times, and in every draw some block names some band exactly 12 times. `obs_count`: 0 marks an empty slot. `land_sea`: 1 marks land. `var_ok`: 1 marks an observed variable.
All inputs are finite; a program needn't handle non-finite values. No bound on the sum of `land_sea` on one device may be relied on, other than what follows from the above.
Results may differ from a plain program's by a relative error of at most 0.0003.
Values sent between devices are 32-bit elements; how exact they have to be, the bound alone decides.
A program may use at most 128 MiB of HBM per device.

v0:
```python
import functools

import jax
import jax.numpy as jnp
from jax import lax
from jax.experimental import pallas as pl
from jax.experimental.pallas import tpu as pltpu
from jax.sharding import PartitionSpec as P

F32 = jnp.float32
BF16 = jnp.bfloat16
CAP = 12
MSG = 2 * CAP
LCAP = 16
SIDE = 8
WIDE = 80
BUF = 88
CHUNK = 512
MESH = pl.DeviceIdType.MESH


def halves(x):
    high = x.astype(BF16)
    return high, (x - high.astype(F32)).astype(BF16)


def nn(a, b):
    return lax.dot_general(a, b, (((1,), (0,)), ((), ())), preferred_element_type=F32)


def nt(a, b):
    return lax.dot_general(a, b, (((1,), (1,)), ((), ())), preferred_element_type=F32)


def gelu_parts(x):
    c = 0.7978845608028654
    t = jnp.tanh(c * (x + 0.044715 * x * x * x))
    return 0.5 * x * (1.0 + t), t


def gelu_slope(x):
    c = 0.7978845608028654
    t = jnp.tanh(c * (x + 0.044715 * x * x * x))
    return 0.5 * (1.0 + t) + 0.5 * x * (1.0 - t * t) * (c * (1.0 + 3.0 * 0.044715 * x * x))


def kernel(
    n_lon, n_lat, slots, patch, variables,
    latent, w1, b1, w2, b2, head, hbias, land, ok, err, band, cell, count, value,
    out,
    lat_ext, sa_hi, sa_lo, w1_v, w1_hi, w1_lo, w2_v, w2_hi, w2_lo, b1_v, b2_v,
    pre1, act1, sb_hi, sb_lo, pre2, head_v, head_hi, head_lo, hb_v, land_v, ok_v, err_v,
    band_v, cell_v, count_v, value_v, scale_v,
    oh, oht, pm, pmt, land_send, land_recv, col_send, col_recv, term_send, term_recv,
    g_ext, sg_hi, sg_lo, p_ext, sp_hi, sp_lo, out_v,
    load_sem, h_send, h_recv, g_send, g_recv, l_send, l_recv, c_send, c_recv, t_send, t_recv,
):
    lon, lat = lax.axis_index("lon"), lax.axis_index("lat")
    north = 1 - lax.div(lat + n_lat - 1, n_lat)
    south = lax.div(lat + 1, n_lat)
    northf, southf = north.astype(F32), south.astype(F32)

    loads = [
        (latent, lat_ext.at[2:10, SIDE:SIDE + 64, :]),
        (band, band_v.at[:, 0:n_lat * slots]),
        (cell, cell_v.at[:, 0:n_lat * slots]),
        (count, count_v.at[:, 0:n_lat * slots]),
        (land, land_v),
        (w1, w1_v),
        (b1, b1_v),
        (w2, w2_v),
        (b2, b2_v),
        (ok, ok_v),
        (err, err_v),
        (hbias, hb_v),
        (head, head_v),
        (value, value_v),
    ]
    copies = [pltpu.make_async_copy(s, d, load_sem.at[i]) for i, (s, d) in enumerate(loads)]
    for copy in copies:
        copy.start()
    (ld_lat, ld_band, ld_cell, ld_count, ld_land, ld_w1, ld_b1, ld_w2, ld_b2, ld_ok, ld_err, ld_hb, ld_head,
     ld_value) = copies

    half = n_lon // 2
    up_lat, down_lat = lat - 1 + north, lat + 1 - south
    around = []
    for dr in (-1, 0, 1):
        for dc in (-1, 0, 1):
            if dr == 0 and dc == 0:
                continue
            turn = half * north if dr < 0 else half * south if dr > 0 else 0
            to_lon = lax.rem(lon + dc + turn + n_lon, n_lon)
            to_lat = up_lat if dr < 0 else down_lat if dr > 0 else lat
            around.append((dr, dc, (to_lon, to_lat)))

    barrier = pltpu.get_barrier_semaphore()
    for _, _, device in around:
        pl.semaphore_signal(barrier, inc=1, device_id=device, device_id_type=MESH)
    for step in range(1, n_lat):
        peer = lax.rem(lat + step, n_lat)
        pl.semaphore_signal(barrier, inc=1, device_id=(lon, peer), device_id_type=MESH)

    def rim(buf, send_sem, recv_sem):
        sent = []
        for number, (dr, dc, device) in enumerate(around):
            src_r = (2, 2) if dr < 0 else (8, 2) if dr > 0 else (2, 8)
            src_c = (SIDE, SIDE) if dc < 0 else (SIDE + 56, SIDE) if dc > 0 else (SIDE, 64)
            dst_c = 72 if dc < 0 else 0 if dc > 0 else SIDE
            if dr < 0:
                dst_r, side = 10 - 10 * north, 2 - 2 * north
            elif dr > 0:
                dst_r, side = 10 * south, 2 * south
            else:
                dst_r, side = 2, 1
            slot = side * 3 + (1 - dc)
            src = buf.at[pl.ds(src_r[0], src_r[1]), pl.ds(src_c[0], src_c[1]), :]
            dst = buf.at[pl.ds(dst_r, src_r[1]), pl.ds(dst_c, src_c[1]), :]
            copy = pltpu.make_async_remote_copy(
                src_ref=src, dst_ref=dst, send_sem=send_sem.at[number], recv_sem=recv_sem.at[slot],
                device_id=device, device_id_type=MESH)
            copy.start()
            sent.append(copy)
        return sent

    def rim_arrived(buf, recv_sem, send_sem):
        for number, (dr, dc, device) in enumerate(around):
            rows = (0, 2) if dr < 0 else (10, 2) if dr > 0 else (2, 8)
            cols = (0, SIDE) if dc < 0 else (72, SIDE) if dc > 0 else (SIDE, 64)
            ref = buf.at[pl.ds(rows[0], rows[1]), pl.ds(cols[0], cols[1]), :]
            slot = (dr + 1) * 3 + dc + 1
            pltpu.make_async_remote_copy(
                src_ref=ref, dst_ref=ref, send_sem=send_sem.at[number], recv_sem=recv_sem.at[slot],
                device_id=device, device_id_type=MESH).wait_recv()

    def exchange(src, dst, send_sem, recv_sem):
        sent = []
        for step in range(1, n_lat):
            peer = lax.rem(lat + step, n_lat)
            copy = pltpu.make_async_remote_copy(
                src_ref=src.at[peer], dst_ref=dst.at[lat], send_sem=send_sem.at[step], recv_sem=recv_sem.at[lat],
                device_id=(lon, peer), device_id_type=MESH)
            copy.start()
            sent.append(copy)
        dst[pl.ds(lat, 1)] = src[pl.ds(lat, 1)]
        return sent

    def arrived(dst, send_sem, recv_sem):
        for step in range(1, n_lat):
            peer = lax.rem(lat + step, n_lat)
            pltpu.make_async_remote_copy(
                src_ref=dst.at[peer], dst_ref=dst.at[peer], send_sem=send_sem.at[step], recv_sem=recv_sem.at[peer],
                device_id=(lon, peer), device_id_type=MESH).wait_recv()

    lat_ext[:, 80:88, :] = jnp.zeros((12, 8, lat_ext.shape[2]), F32)
    g_ext[:, 80:88, :] = jnp.zeros((12, 8, g_ext.shape[2]), F32)

    pl.semaphore_wait(barrier, len(around) + n_lat - 1)
    ld_lat.wait()
    rim1 = rim(lat_ext, h_send, h_recv)

    ld_band.wait()
    ld_cell.wait()
    ld_count.wait()
    lane = lax.broadcasted_iota(jnp.int32, (n_lat, 128), 1)
    live = lane < slots

    def blocks(ref):
        row = ref[...]
        return jnp.concatenate([row[:, slots * a:slots * a + 128] for a in range(n_lat)], axis=0)

    bands, cells, counts = blocks(band_v), blocks(cell_v), blocks(count_v)
    below = (lax.broadcasted_iota(jnp.int32, (128, 128), 0) < lax.broadcasted_iota(jnp.int32, (128, 128), 1))
    below = below.astype(F32).astype(BF16)
    mine = jnp.where(live & (bands == lat), 1.0, 0.0)
    rank = nn(mine.astype(BF16), below)
    pick = jnp.where(mine > 0.0, rank, -1.0)
    cellsf = cells.astype(F32) + 1.0
    msg_k = lax.rem(lax.broadcasted_iota(jnp.int32, (MSG, 128), 0), CAP).astype(F32)
    land_k = lax.broadcasted_iota(jnp.int32, (LCAP, 128), 0).astype(F32)
    named, named_land = [], []
    for a in range(n_lat):
        p, c = pick[a:a + 1], cellsf[a:a + 1]
        named.append(jnp.sum(jnp.where(p == msg_k, c, 0.0), axis=1, keepdims=True))
        named_land.append(jnp.sum(jnp.where(p == land_k, c, 0.0), axis=1, keepdims=True))
    wanted = jnp.concatenate(named, axis=0).astype(jnp.int32) - 1
    wanted_land = jnp.concatenate(named_land, axis=0).astype(jnp.int32) - 1
    rows = n_lat * MSG
    oh[...] = jnp.where(wanted == lax.broadcasted_iota(jnp.int32, (rows, 512), 1), 1.0, 0.0).astype(BF16)
    wanted_row = jnp.transpose(jnp.broadcast_to(wanted.astype(F32), (rows, 128)))[0:1, :].astype(jnp.int32)
    oht[...] = jnp.where(wanted_row == lax.broadcasted_iota(jnp.int32, (512, rows), 0), 1.0, 0.0).astype(BF16)

    own = lax.broadcasted_iota(jnp.int32, (n_lat, 128), 0) == lat
    own_band = jnp.sum(jnp.where(own, bands, 0), axis=0, keepdims=True)
    own_count = jnp.sum(jnp.where(own, counts, 0), axis=0, keepdims=True)
    theirs = jnp.where(live & (own_band == lax.broadcasted_iota(jnp.int32, (n_lat, 128), 0)), 1.0, 0.0)
    place = jnp.where(theirs > 0.0, nn(theirs.astype(BF16), below), -1.0)
    pmt_f = jnp.concatenate([jnp.where(place[b:b + 1] == msg_k, 1.0, 0.0) for b in range(n_lat)], axis=0)
    pmt[...] = pmt_f.astype(BF16)
    pm[...] = jnp.transpose(pmt_f).astype(BF16)
    pml = jnp.concatenate([jnp.where(place[b:b + 1] == land_k, 1.0, 0.0) for b in range(n_lat)], axis=0)
    pml = jnp.transpose(pml).astype(BF16)
    weight = jnp.transpose(jnp.broadcast_to(own_count.astype(F32) * 0.125, (128, 128)))[:slots, 0:1]

    ld_land.wait()
    lrows = n_lat * LCAP
    land_b = land_v[...].astype(F32).astype(BF16)
    tile_row, tile_col = wanted_land >> 6, wanted_land & 63
    valid = wanted_land >= 0
    tile_row = jnp.where(valid, tile_row, -1000)
    in_tile = (lax.broadcasted_iota(jnp.int32, (lrows, 512), 1) >> 3) == tile_col
    flags = jnp.zeros((lrows, 128), F32)
    for p in range(8):
        pick_row = (lax.broadcasted_iota(jnp.int32, (lrows, 64), 1) == tile_row * 8 + p)
        found = nn(jnp.where(pick_row, 1.0, 0.0).astype(BF16), land_b)
        found = jnp.where(in_tile, found, 0.0).astype(BF16)
        col = lax.broadcasted_iota(jnp.int32, (512, 128), 1)
        fold = (lax.broadcasted_iota(jnp.int32, (512, 128), 0) & 7) + 8 * p == col
        flags = flags + nn(found, jnp.where(fold, 1.0, 0.0).astype(BF16))
    on_land = jnp.concatenate([flags[:, :64], jnp.where(valid, 1.0 - flags[:, :64], 0.0)], axis=1)
    land_send[...] = on_land.reshape(n_lat, LCAP, 128)
    land_sent = exchange(land_send, land_recv, l_send, l_recv)

    ld_w1.wait()
    high, low = halves(w1_v[...])
    w1_hi[...] = high
    w1_lo[...] = low
    ld_w2.wait()
    high, low = halves(w2_v[...])
    w2_hi[...] = high
    w2_lo[...] = low
    ld_b1.wait()
    ld_b2.wait()

    rim_arrived(lat_ext, h_recv, h_send)
    for j in range(3):
        span = slice(SIDE - 2 + j, SIDE - 2 + j + WIDE)
        for at, source, length in ((0, north, 1), (1, 1 - north, 1), (2, 2, 8), (10, 10 + south, 1), (11, 11 - south, 1)):
            high, low = halves(lat_ext[pl.ds(source, length), span, :])
            sa_hi[j, at:at + length] = high
            sa_lo[j, at:at + length] = low

    def taps1(ref):
        parts = []
        for i in range(3):
            for j in range(3):
                if i == 1:
                    rows_ = ref[j, 1:11]
                else:
                    first = 2 * north if i == 0 else 2 - 2 * north
                    last = 9 + 2 * south if i == 0 else 11 - 2 * south
                    rows_ = jnp.concatenate(
                        [ref[j, pl.ds(first, 1)], ref[j, 1 + i:9 + i], ref[j, pl.ds(last, 1)]], axis=0)
                parts.append(rows_.reshape(10 * WIDE, rows_.shape[2]))
        return jnp.concatenate(parts, axis=1)

    k1 = w1_v.shape[1]
    hid = w1_v.shape[2]
    wh = w1_hi[...].reshape(9 * k1, hid)
    wl = w1_lo[...].reshape(9 * k1, hid)
    lhs = taps1(sa_hi)
    summed = nn(lhs, wh) + nn(lhs, wl) + nn(taps1(sa_lo), wh) + b1_v[...]
    pre1[...] = summed.reshape(10, WIDE, hid)
    act1[...] = gelu_parts(summed)[0].reshape(10, WIDE, hid)

    for j in range(3):
        high, low = halves(act1[:, j:j + 64, :])
        sb_hi[j] = high
        sb_lo[j] = low

    def taps2(ref):
        return jnp.concatenate([ref[j, i:i + 8].reshape(512, hid) for i in range(3) for j in range(3)], axis=1)

    wh = w2_hi[...].reshape(9 * hid, hid)
    wl = w2_lo[...].reshape(9 * hid, hid)
    lhs = taps2(sb_hi)
    summed = nn(lhs, wh) + nn(lhs, wl) + nn(taps2(sb_lo), wh) + b2_v[...]
    pre2[...] = summed
    act2, _ = gelu_parts(summed)

    upper = lax.rem(lax.broadcasted_iota(jnp.int32, (rows, 128), 0), MSG) < CAP

    def fold_halves(x):
        return jnp.where(upper, x[:, :128], x[:, 128:])

    def unfold(x):
        return jnp.concatenate([jnp.where(upper, x, 0.0), jnp.where(upper, 0.0, x)], axis=1)

    high, low = halves(act2)
    sent_cols = nn(oh[...], jnp.concatenate([high, low], axis=1))
    col_send[...] = fold_halves(sent_cols[:, :hid] + sent_cols[:, hid:]).reshape(n_lat, MSG, 128)
    cols_sent = exchange(col_send, col_recv, c_send, c_recv)

    ld_head.wait()
    high, low = halves(head_v[...])
    head_hi[...] = high
    head_lo[...] = low
    ld_ok.wait()
    ld_err.wait()
    ld_hb.wait()
    ld_value.wait()
    arrived(land_recv, l_send, l_recv)
    flags_own = nn(pml, land_recv[...].reshape(lrows, 128).astype(BF16))[:slots].astype(BF16)
    inv = 1.0 / (err_v[...] * err_v[...])
    inv_hi = inv.astype(BF16).astype(F32)
    inv_mid = (inv - inv_hi).astype(BF16).astype(F32)
    inv_lo = inv - inv_hi - inv_mid
    okf = ok_v[...].astype(F32)
    kind = lax.broadcasted_iota(jnp.int32, (16, variables), 0)
    table = jnp.where(kind == 0, inv_hi, jnp.where(kind == 1, inv_mid, jnp.where(kind == 2, inv_lo, 0.0)))
    table = table + jnp.where(kind == 3, okf[1:2], 0.0) + jnp.where(kind == 4, okf[0:1], 0.0)
    table = table.astype(BF16)
    spans = [(at, min(CHUNK, patch - at)) for at in range(0, patch, CHUNK)]
    for at, size in spans:
        place_ = lax.broadcasted_iota(jnp.int32, (1, size), 1) + at
        pixel = ((place_.astype(F32) + 0.5) * (1.0 / variables)).astype(jnp.int32)
        variable = place_ - pixel * variables
        spread = nn(table, jnp.where(lax.broadcasted_iota(jnp.int32, (variables, size), 0) == variable, 1.0, 0.0).astype(BF16))
        inv_row = spread[0:1] + spread[1:2] + spread[2:3]
        which = lax.broadcasted_iota(jnp.int32, (128, size), 0)
        ok_rows = jnp.where(which == pixel, spread[3:4], jnp.where(which == pixel + 64, spread[4:5], 0.0))
        allowed = nn(flags_own, ok_rows.astype(BF16))
        scale_v[:, at:at + size] = weight * inv_row * allowed
        value_v[:, at:at + size] = value_v[:, at:at + size] - hb_v[:, at:at + size]

    arrived(col_recv, c_send, c_recv)
    high, low = halves(unfold(col_recv[...].reshape(rows, 128)))
    cols = nn(pm[...], jnp.concatenate([high, low], axis=1))[:slots].astype(BF16)
    cols_hi, cols_lo = cols[:, :hid], cols[:, hid:]
    cols_both = jnp.concatenate([cols_hi, cols_lo], axis=0)
    terms = jnp.zeros((slots, hid), F32)
    for at, size in spans:
        hh, hl = head_hi[at:at + size, :], head_lo[at:at + size, :]
        both = nt(cols_both, hh)
        decoded = both[:slots] + both[slots:] + nt(cols_hi, hl)
        scaled = scale_v[:, at:at + size] * (decoded - value_v[:, at:at + size])
        high, low = halves(scaled)
        both = nn(jnp.concatenate([high, low], axis=0), hh)
        terms = terms + both[:slots] + both[slots:] + nn(high, hl)
    high, low = halves(terms)
    both = jnp.concatenate([high, low], axis=1)
    if slots < 128:
        both = jnp.concatenate([both, jnp.zeros((128 - slots, 2 * hid), BF16)], axis=0)
    sent_terms = nn(pmt[...], both)
    term_send[...] = fold_halves(sent_terms[:, :hid] + sent_terms[:, hid:]).reshape(n_lat, MSG, 128)
    terms_sent = exchange(term_send, term_recv, t_send, t_recv)

    pre2[...] = gelu_slope(pre2[...])
    pre1[...] = gelu_slope(pre1[...])

    arrived(term_recv, t_send, t_recv)
    high, low = halves(unfold(term_recv[...].reshape(rows, 128)))
    hidden = nn(oht[...], jnp.concatenate([high, low], axis=1))
    grad2 = (hidden[:, :hid] + hidden[:, hid:]) * pre2[...]
    g_ext[2:10, SIDE:SIDE + 64, :] = grad2.reshape(8, 64, hid)
    rim2 = rim(g_ext, g_send, g_recv)
    rim_arrived(g_ext, g_recv, g_send)

    for j in range(3):
        span = slice(SIDE - j, SIDE - j + WIDE)

        def row(at, length=1):
            return g_ext[pl.ds(at, length), span, :]

        r0, r1, r10, r11 = row(north), row(1 - north), row(10 + south), row(11 - south)
        pieces = (
            (0, r0), (1, r1), (2, row(2, 8)), (10, r10), (11, r11),
            (12, row(2) + northf * r0), (13, row(3) + northf * r1),
            (14, r10 * (1.0 - southf)), (15, r11 * (1.0 - southf)),
            (16, r0 * (1.0 - northf)), (17, r1 * (1.0 - northf)),
            (18, row(8) + southf * r10), (19, row(9) + southf * r11),
        )
        for at, piece in pieces:
            high, low = halves(piece)
            sg_hi[j, at:at + piece.shape[0]] = high
            sg_lo[j, at:at + piece.shape[0]] = low

    def taps3(ref):
        parts = []
        for i in range(3):
            for j in range(3):
                if i == 0:
                    rows_ = jnp.concatenate([ref[j, 12:14], ref[j, 4:10], ref[j, 14:16]], axis=0)
                elif i == 1:
                    rows_ = ref[j, 1:11]
                else:
                    rows_ = jnp.concatenate([ref[j, 16:18], ref[j, 2:8], ref[j, 18:20]], axis=0)
                parts.append(rows_.reshape(10 * WIDE, hid))
        return jnp.concatenate(parts, axis=1)

    wh = jnp.concatenate([w2_hi[t] for t in range(9)], axis=1)
    wl = jnp.concatenate([w2_lo[t] for t in range(9)], axis=1)
    lhs = taps3(sg_hi)
    grad1 = nt(lhs, wh) + nt(lhs, wl) + nt(taps3(sg_lo), wh)
    p_ext[...] = grad1.reshape(10, WIDE, hid) * pre1[...]

    for j in range(3):
        span = slice(2 - j, 2 - j + 64)
        q0, q9 = p_ext[0:1, span, :], p_ext[9:10, span, :]
        pieces = (
            (0, p_ext[:, span, :]),
            (10, p_ext[2:3, span, :] + northf * q0), (11, q9 * (1.0 - southf)),
            (12, q0 * (1.0 - northf)), (13, p_ext[7:8, span, :] + southf * q9),
        )
        for at, piece in pieces:
            high, low = halves(piece)
            sp_hi[j, at:at + piece.shape[0]] = high
            sp_lo[j, at:at + piece.shape[0]] = low

    def taps4(ref):
        parts = []
        for i in range(3):
            for j in range(3):
                if i == 0:
                    rows_ = jnp.concatenate([ref[j, 10:11], ref[j, 3:9], ref[j, 11:12]], axis=0)
                elif i == 1:
                    rows_ = ref[j, 1:9]
                else:
                    rows_ = jnp.concatenate([ref[j, 12:13], ref[j, 1:7], ref[j, 13:14]], axis=0)
                parts.append(rows_.reshape(512, hid))
        return jnp.concatenate(parts, axis=1)

    wh = jnp.concatenate([w1_hi[t] for t in range(9)], axis=1)
    wl = jnp.concatenate([w1_lo[t] for t in range(9)], axis=1)
    both = nt(taps4(sp_hi), jnp.concatenate([wh, wl], axis=0))
    result = both[:, :k1] + both[:, k1:] + nt(taps4(sp_lo), wh)
    out_v[...] = result.reshape(8, 64, k1)
    done = pltpu.make_async_copy(out_v, out, load_sem.at[0])
    done.start()
    for copy in rim1 + land_sent + cols_sent + terms_sent + rim2:
        copy.wait_send()
    done.wait()


def shards(n_lon, n_lat, latent, conv1_weight, conv1_bias, conv2_weight, conv2_bias, head_weight, head_bias, land_sea,
           var_ok, obs_error, obs_band, obs_cell, obs_count, obs_value):
    lc, hid = conv1_weight.shape[2], conv1_weight.shape[3]
    slots, patch = obs_value.shape[1], obs_value.shape[2]
    variables = var_ok.shape[1]
    listed = n_lat * slots
    padded = -(-(listed + 128) // 128) * 128
    vmem = pltpu.VMEM
    rows = n_lat * MSG
    scratch = [
        vmem((12, BUF, lc), F32),
        vmem((3, 12, WIDE, lc), BF16), vmem((3, 12, WIDE, lc), BF16),
        vmem((9, lc, hid), F32), vmem((9, lc, hid), BF16), vmem((9, lc, hid), BF16),
        vmem((9, hid, hid), F32), vmem((9, hid, hid), BF16), vmem((9, hid, hid), BF16),
        vmem((1, hid), F32), vmem((1, hid), F32),
        vmem((10, WIDE, hid), F32), vmem((10, WIDE, hid), F32),
        vmem((3, 10, 64, hid), BF16), vmem((3, 10, 64, hid), BF16),
        vmem((512, hid), F32),
        vmem((patch, hid), F32), vmem((patch, hid), BF16), vmem((patch, hid), BF16),
        vmem((1, patch), F32), vmem(land_sea.shape, jnp.int32), vmem(var_ok.shape, jnp.int32),
        vmem((1, variables), F32),
        vmem((1, padded), jnp.int32), vmem((1, padded), jnp.int32), vmem((1, padded), jnp.int32),
        vmem((slots, patch), F32), vmem((slots, patch), F32),
        vmem((rows, 512), BF16), vmem((512, rows), BF16),
        vmem((128, rows), BF16), vmem((rows, 128), BF16),
        vmem((n_lat, LCAP, 128), F32), vmem((n_lat, LCAP, 128), F32),
        vmem((n_lat, MSG, 128), F32), vmem((n_lat, MSG, 128), F32),
        vmem((n_lat, MSG, 128), F32), vmem((n_lat, MSG, 128), F32),
        vmem((12, BUF, hid), F32),
        vmem((3, 20, WIDE, hid), BF16), vmem((3, 20, WIDE, hid), BF16),
        vmem((10, WIDE, hid), F32),
        vmem((3, 14, 64, hid), BF16), vmem((3, 14, 64, hid), BF16),
        vmem((8, 64, lc), F32),
        pltpu.SemaphoreType.DMA((14,)),
        pltpu.SemaphoreType.DMA((8,)), pltpu.SemaphoreType.DMA((9,)),
        pltpu.SemaphoreType.DMA((8,)), pltpu.SemaphoreType.DMA((9,)),
    ] + [pltpu.SemaphoreType.DMA((n_lat,))] * 6
    return pl.pallas_call(
        functools.partial(kernel, n_lon, n_lat, slots, patch, variables),
        out_shape=jax.ShapeDtypeStruct(latent.shape, F32),
        in_specs=[pl.BlockSpec(memory_space=pl.ANY)] * 14,
        out_specs=pl.BlockSpec(memory_space=pl.ANY),
        scratch_shapes=scratch,
        compiler_params=pltpu.CompilerParams(
            collective_id=0, has_side_effects=True, vmem_limit_bytes=60 * 1024 * 1024),
    )(latent, conv1_weight.reshape(9, lc, hid), conv1_bias.reshape(1, hid), conv2_weight.reshape(9, hid, hid),
      conv2_bias.reshape(1, hid), head_weight.T, head_bias.reshape(1, patch), land_sea, var_ok,
      obs_error.reshape(1, variables), obs_band.reshape(1, listed), obs_cell, obs_count, obs_value[0])


def solution(mesh):
    in_specs = (
        P("lat", "lon", None),
        P(),
        P(),
        P(),
        P(),
        P(),
        P(),
        P("lat", "lon"),
        P(),
        P(),
        P("lon", None, None),
        P("lon", None),
        P("lon", None),
        P("lon", "lat", None),
    )
    out_specs = P("lat", "lon", None)
    body = functools.partial(shards, mesh.shape["lon"], mesh.shape["lat"])
    return jax.shard_map(body, mesh=mesh, in_specs=in_specs, out_specs=out_specs, check_vma=False)
```

profile of v0, /device:TPU:1, one launch (start us, length us, event | category | flops | bytes accessed | tf_op | source)
XLA Modules:
  0.0 62.4 jit_solution(3894184939686817939)
XLA Ops:
  0.0 1.3 %reshape.25.hbias = f32[1,4416]{1,0:T(1,128)} reshape(f32[4416]{0:T(1024)} %param.20) | data formatting | bytes 35328 | tf_op jit(solution)/shard_map/reshape | solution.py:481
  1.3 59.4 %shard_map.136 = f32[8,64,128]{2,1,0:T(8,128)} custom-call(f32[8,64,128]{2,1,0:T(8,128)} %latent.1, f32[9,128,256]{2,1,0:T(8,128)} %bitcast.11, f32[1,256]{1,0:T(1,128)} %bitcast.13, f32[9,256,256]{2,1,0:T(8,128)} %bitcast.9, f32[1,256]{1,0:T(1,128)} %bitcast.14, f32[4416,256]{1,0:T(8,128)} %bitcast.8, f32[1,4416]{1,0:T(1,128)} %reshape.25.hbias, ...), custom_call_target="tpu_custom_call" | custom-call | tf_op jit(solution)/shard_map/pallas_call | solution.py:472
  60.8 1.7 %copy.16 = f32[8,64,128]{2,1,0:T(8,128)} copy(f32[8,64,128]{2,1,0:T(8,128)} %shard_map.136) | data formatting | bytes 524288
where the time goes:
time: 62.6 us; the launch traced here: 62.4 us
  Pallas kernels  59.4 us (95%)
  local copies, waits for them, and re-layouts  3.02 us (5%)
    pallas_call x1, Pallas kernels, shards(): pl.pallas_call(functools.partial(kernel, n_lon, n_lat, slots, patch, vari...  59.4 us
    unnamed x1, local copies, waits for them, and re-layouts  1.67 us
    reshape x1, local copies, waits for them, and re-layouts, shards(): head_bias.reshape(1, patch)  1.34 us

commit v1 on v0

v1 whole, which is shorter than its diff:
```python
import functools

import jax
import jax.numpy as jnp
from jax import lax
from jax.experimental import pallas as pl
from jax.experimental.pallas import tpu as pltpu
from jax.sharding import PartitionSpec as P

F32 = jnp.float32
BF16 = jnp.bfloat16
CAP = 12
MSG = 2 * CAP
LCAP = 16
SIDE = 8
WIDE = 80
BUF = 88
CHUNK = 512
MESH = pl.DeviceIdType.MESH


def halves(x):
    high = x.astype(BF16)
    return high, (x - high.astype(F32)).astype(BF16)


def nn(a, b):
    return lax.dot_general(a, b, (((1,), (0,)), ((), ())), preferred_element_type=F32)


def nt(a, b):
    return lax.dot_general(a, b, (((1,), (1,)), ((), ())), preferred_element_type=F32)


def gelu_parts(x):
    c = 0.7978845608028654
    t = jnp.tanh(c * (x + 0.044715 * x * x * x))
    return 0.5 * x * (1.0 + t), t


def gelu_slope(x):
    c = 0.7978845608028654
    t = jnp.tanh(c * (x + 0.044715 * x * x * x))
    return 0.5 * (1.0 + t) + 0.5 * x * (1.0 - t * t) * (c * (1.0 + 3.0 * 0.044715 * x * x))


def kernel(
    n_lon, n_lat, slots, patch, variables,
    latent, w1, b1, w2, b2, head, hbias, land, ok, err, band, cell, count, value,
    out,
    lat_ext, sa_hi, sa_lo, w1_v, w1_hi, w1_lo, w2_v, w2_hi, w2_lo, b1_v, b2_v,
    pre1, act1, sb_hi, sb_lo, pre2, head_v, head_hi, head_lo, hb_v, land_v, ok_v, err_v,
    band_v, cell_v, count_v, value_v, ok_rows, inv_row,
    oh, oht, oht_msg, pmt, land_send, land_recv, term_send, term_recv,
    g_ext, sg_hi, sg_lo, p_ext, sp_hi, sp_lo, out_v,
    load_sem, h_send, h_recv, g_send, g_recv, l_send, l_recv, t_send, t_recv,
):
    lon, lat = lax.axis_index("lon"), lax.axis_index("lat")
    north = 1 - lax.div(lat + n_lat - 1, n_lat)
    south = lax.div(lat + 1, n_lat)
    northf, southf = north.astype(F32), south.astype(F32)
    hid = w1_v.shape[1]
    k1 = lat_ext.shape[2]

    loads = [
        (band, band_v.at[:, 0:n_lat * slots]),
        (cell, cell_v.at[:, 0:n_lat * slots]),
        (count, count_v.at[:, 0:n_lat * slots]),
        (land, land_v),
        (latent, lat_ext.at[2:10, SIDE:SIDE + 64, :]),
        (w1, w1_v),
        (b1, b1_v),
        (ok, ok_v),
        (err, err_v),
        (hbias, hb_v),
        (w2, w2_v),
        (b2, b2_v),
        (value, value_v),
        (head, head_v),
    ]
    copies = [pltpu.make_async_copy(s, d, load_sem.at[i]) for i, (s, d) in enumerate(loads)]
    (ld_band, ld_cell, ld_count, ld_land, ld_lat, ld_w1, ld_b1, ld_ok, ld_err, ld_hb, ld_w2, ld_b2, ld_value,
     ld_head) = copies
    for copy in copies[:5]:
        copy.start()

    half = n_lon // 2
    up_lat, down_lat = lat - 1 + north, lat + 1 - south
    around = []
    for dr in (-1, 0, 1):
        for dc in (-1, 0, 1):
            if dr == 0 and dc == 0:
                continue
            turn = half * north if dr < 0 else half * south if dr > 0 else 0
            to_lon = lax.rem(lon + dc + turn + n_lon, n_lon)
            to_lat = up_lat if dr < 0 else down_lat if dr > 0 else lat
            around.append((dr, dc, (to_lon, to_lat)))

    deep = n_lat // 2
    steps = [(far, step) for far in range(2) for step in range(deep) if far or step]
    steps.sort(key=lambda s: -(2 * s[0] + min(s[1], deep - s[1])))
    peers = [lax.rem(lax.div(lat, deep) + far, 2) * deep + lax.rem(lax.rem(lat, deep) + step, deep)
             for far, step in steps]

    barrier = pltpu.get_barrier_semaphore()
    for peer in peers:
        pl.semaphore_signal(barrier, inc=1, device_id=(lon, peer), device_id_type=MESH)
    for _, _, device in around:
        pl.semaphore_signal(barrier, inc=1, device_id=device, device_id_type=MESH)
    for copy in copies[5:]:
        copy.start()

    def rim(buf, send_sem, recv_sem):
        sent = []
        for number, (dr, dc, device) in enumerate(around):
            src_r = (2, 2) if dr < 0 else (8, 2) if dr > 0 else (2, 8)
            src_c = (SIDE, SIDE) if dc < 0 else (SIDE + 56, SIDE) if dc > 0 else (SIDE, 64)
            dst_c = 72 if dc < 0 else 0 if dc > 0 else SIDE
            if dr < 0:
                dst_r, side = 10 - 10 * north, 2 - 2 * north
            elif dr > 0:
                dst_r, side = 10 * south, 2 * south
            else:
                dst_r, side = 2, 1
            slot = side * 3 + (1 - dc)
            src = buf.at[pl.ds(src_r[0], src_r[1]), pl.ds(src_c[0], src_c[1]), :]
            dst = buf.at[pl.ds(dst_r, src_r[1]), pl.ds(dst_c, src_c[1]), :]
            copy = pltpu.make_async_remote_copy(
                src_ref=src, dst_ref=dst, send_sem=send_sem.at[number], recv_sem=recv_sem.at[slot],
                device_id=device, device_id_type=MESH)
            copy.start()
            sent.append(copy)
        return sent

    def rim_arrived(buf, recv_sem, send_sem):
        for number, (dr, dc, device) in enumerate(around):
            rows_ = (0, 2) if dr < 0 else (10, 2) if dr > 0 else (2, 8)
            cols_ = (0, SIDE) if dc < 0 else (72, SIDE) if dc > 0 else (SIDE, 64)
            ref = buf.at[pl.ds(rows_[0], rows_[1]), pl.ds(cols_[0], cols_[1]), :]
            slot = (dr + 1) * 3 + dc + 1
            pltpu.make_async_remote_copy(
                src_ref=ref, dst_ref=ref, send_sem=send_sem.at[number], recv_sem=recv_sem.at[slot],
                device_id=device, device_id_type=MESH).wait_recv()

    def exchange(src, dst, send_sem, recv_sem):
        sent = []
        for number, peer in enumerate(peers):
            copy = pltpu.make_async_remote_copy(
                src_ref=src.at[peer], dst_ref=dst.at[lat], send_sem=send_sem.at[number], recv_sem=recv_sem.at[lat],
                device_id=(lon, peer), device_id_type=MESH)
            copy.start()
            sent.append(copy)
        dst[pl.ds(lat, 1)] = src[pl.ds(lat, 1)]
        return sent

    def arrived(dst, send_sem, recv_sem):
        for number, peer in enumerate(peers):
            pltpu.make_async_remote_copy(
                src_ref=dst.at[peer], dst_ref=dst.at[peer], send_sem=send_sem.at[number], recv_sem=recv_sem.at[peer],
                device_id=(lon, peer), device_id_type=MESH).wait_recv()

    def split(src, high_ref, low_ref, step):
        def body(i, carry):
            at = pl.ds(pl.multiple_of(i * step, step), step)
            high, low = halves(src[at, :])
            high_ref[at, :] = high
            low_ref[at, :] = low
            return carry
        lax.fori_loop(0, src.shape[0] // step, body, 0)

    lat_ext[:, 80:88, :] = jnp.zeros((12, 8, k1), F32)
    g_ext[:, 80:88, :] = jnp.zeros((12, 8, hid), F32)

    ld_band.wait()
    ld_cell.wait()
    ld_count.wait()
    lane = lax.broadcasted_iota(jnp.int32, (n_lat, 128), 1)
    live = lane < slots

    def blocks(ref):
        row = ref[...]
        return jnp.concatenate([row[:, slots * a:slots * a + 128] for a in range(n_lat)], axis=0)

    bands, cells, counts = blocks(band_v), blocks(cell_v), blocks(count_v)
    below = (lax.broadcasted_iota(jnp.int32, (128, 128), 0) < lax.broadcasted_iota(jnp.int32, (128, 128), 1))
    below = below.astype(F32).astype(BF16)
    mine = jnp.where(live & (bands == lat), 1.0, 0.0)
    pick = jnp.where(mine > 0.0, nn(mine.astype(BF16), below), -1.0)
    cellsf = cells.astype(F32) + 1.0
    countsf = counts.astype(F32) * 0.125
    msg_k = lax.rem(lax.broadcasted_iota(jnp.int32, (MSG, 128), 0), CAP).astype(F32)
    first = lax.broadcasted_iota(jnp.int32, (MSG, 128), 0) < CAP
    taken = n_lat * CAP
    named, merged = [], []
    for q in range(n_lat // 2):
        def two(x):
            return jnp.where(first, x[2 * q:2 * q + 1], x[2 * q + 1:2 * q + 2])
        hit = two(pick) == msg_k
        named.append(jnp.sum(jnp.where(hit, two(cellsf), 0.0), axis=1, keepdims=True))
        merged.append(jnp.sum(jnp.where(hit, two(countsf), 0.0), axis=1, keepdims=True))
    wanted = jnp.concatenate(named, axis=0).astype(jnp.int32) - 1
    weight = jnp.concatenate(merged, axis=0)
    oh[...] = jnp.where(wanted == lax.broadcasted_iota(jnp.int32, (taken, 512), 1), 1.0, 0.0).astype(BF16)

    ld_land.wait()
    fold = (lax.broadcasted_iota(jnp.int32, (64, 512), 1) >> 3) == lax.broadcasted_iota(jnp.int32, (64, 512), 0)
    fold = jnp.where(fold, 1.0, 0.0).astype(BF16)
    kept = (lax.broadcasted_iota(jnp.int32, (8, 512), 1) & 7) == lax.broadcasted_iota(jnp.int32, (8, 512), 0)
    tiles = []
    for r in range(8):
        strip = land_v[8 * r:8 * r + 8, :].astype(F32)
        spread = jnp.concatenate([jnp.where(kept, strip[p:p + 1], 0.0) for p in range(8)], axis=0)
        tiles.append(nt(fold, spread.astype(BF16)))
    tiles = jnp.concatenate(tiles, axis=0)
    tiles = jnp.concatenate([tiles, 1.0 - tiles], axis=1).astype(BF16)
    flags = nn(oh[...], tiles)
    lrows = n_lat * LCAP
    row = lax.broadcasted_iota(jnp.int32, (lrows, taken), 0)
    into = (row & (LCAP - 1)) + (row >> 4) * CAP == lax.broadcasted_iota(jnp.int32, (lrows, taken), 1)
    into = into & ((row & (LCAP - 1)) < CAP)
    land_send[...] = nn(jnp.where(into, 1.0, 0.0).astype(BF16), flags.astype(BF16)).reshape(n_lat, LCAP, 128)
    flags_w = (flags * weight).astype(BF16)

    pl.semaphore_wait(barrier, len(around) + len(peers))
    land_sent = exchange(land_send, land_recv, l_send, l_recv)
    ld_lat.wait()
    rim1 = rim(lat_ext, h_send, h_recv)

    ld_w1.wait()
    split(w1_v, w1_hi, w1_lo, 128)

    own = lax.broadcasted_iota(jnp.int32, (n_lat, 128), 0) == lat
    own_band = jnp.sum(jnp.where(own, bands, 0), axis=0, keepdims=True)
    own_count = jnp.sum(jnp.where(own, countsf, 0.0), axis=0, keepdims=True)
    theirs = jnp.where(live & (own_band == lax.broadcasted_iota(jnp.int32, (n_lat, 128), 0)), 1.0, 0.0)
    place = jnp.where(theirs > 0.0, nn(theirs.astype(BF16), below), -1.0)
    land_k = lax.broadcasted_iota(jnp.int32, (LCAP, 128), 0).astype(F32)
    pmt[...] = jnp.concatenate(
        [jnp.where(place[b:b + 1] == msg_k, 1.0, 0.0) for b in range(n_lat)], axis=0).astype(BF16)
    pml = jnp.concatenate([jnp.where(place[b:b + 1] == land_k, 1.0, 0.0) for b in range(n_lat)], axis=0)
    pml = jnp.transpose(pml).astype(BF16)
    own_weight = jnp.transpose(jnp.broadcast_to(own_count, (128, 128)))[:, 0:1]

    ld_ok.wait()
    ld_err.wait()
    ld_hb.wait()
    ld_w2.wait()
    split(w2_v, w2_hi, w2_lo, 128)
    inv = 1.0 / (err_v[...] * err_v[...])
    inv_hi = inv.astype(BF16).astype(F32)
    inv_mid = (inv - inv_hi).astype(BF16).astype(F32)
    inv_lo = inv - inv_hi - inv_mid
    okf = ok_v[...].astype(F32)
    kind = lax.broadcasted_iota(jnp.int32, (16, variables), 0)
    table = jnp.where(kind == 0, inv_hi, jnp.where(kind == 1, inv_mid, jnp.where(kind == 2, inv_lo, 0.0)))
    table = table + jnp.where(kind == 3, okf[1:2], 0.0) + jnp.where(kind == 4, okf[0:1], 0.0)
    table = table.astype(BF16)
    spans = [(at, min(CHUNK, patch - at)) for at in range(0, patch, CHUNK)]
    for at, size in spans:
        place_ = lax.broadcasted_iota(jnp.int32, (1, size), 1) + at
        pixel = ((place_.astype(F32) + 0.5) * (1.0 / variables)).astype(jnp.int32)
        variable = place_ - pixel * variables
        chosen = lax.broadcasted_iota(jnp.int32, (variables, size), 0) == variable
        spread = nn(table, jnp.where(chosen, 1.0, 0.0).astype(BF16))
        inv_row[:, at:at + size] = spread[0:1] + spread[1:2] + spread[2:3]
        which = lax.broadcasted_iota(jnp.int32, (128, size), 0)
        seen = jnp.where(which == pixel, spread[3:4], jnp.where(which == pixel + 64, spread[4:5], 0.0))
        ok_rows[:, at:at + size] = seen.astype(BF16)
    ld_b1.wait()
    ld_b2.wait()
    ld_value.wait()
    ld_head.wait()
    split(head_v, head_hi, head_lo, 96)

    rim_arrived(lat_ext, h_recv, h_send)

    for j in range(3):
        span = slice(SIDE - 2 + j, SIDE - 2 + j + WIDE)
        for at, source, length in ((0, north, 1), (1, 1 - north, 1), (2, 2, 8), (10, 10 + south, 1), (11, 11 - south, 1)):
            high, low = halves(lat_ext[pl.ds(source, length), span, :])
            sa_hi[j, at:at + length] = high
            sa_lo[j, at:at + length] = low

    def taps1(ref):
        parts = []
        for i in range(3):
            for j in range(3):
                if i == 1:
                    rows_ = ref[j, 1:11]
                else:
                    first = 2 * north if i == 0 else 2 - 2 * north
                    last = 9 + 2 * south if i == 0 else 11 - 2 * south
                    rows_ = jnp.concatenate(
                        [ref[j, pl.ds(first, 1)], ref[j, 1 + i:9 + i], ref[j, pl.ds(last, 1)]], axis=0)
                parts.append(rows_.reshape(10 * WIDE, rows_.shape[2]))
        return jnp.concatenate(parts, axis=1)

    wh, wl = w1_hi[...], w1_lo[...]
    lhs = taps1(sa_hi)
    summed = nn(lhs, wh) + nn(lhs, wl) + nn(taps1(sa_lo), wh) + b1_v[...]
    pre1[...] = summed.reshape(10, WIDE, hid)
    act1[...] = gelu_parts(summed)[0].reshape(10, WIDE, hid)

    for j in range(3):
        high, low = halves(act1[:, j:j + 64, :])
        sb_hi[j] = high
        sb_lo[j] = low

    def taps2(ref):
        return jnp.concatenate([ref[j, i:i + 8].reshape(512, hid) for i in range(3) for j in range(3)], axis=1)

    wh, wl = w2_hi[...], w2_lo[...]
    lhs = taps2(sb_hi)
    summed = nn(lhs, wh) + nn(lhs, wl) + nn(taps2(sb_lo), wh) + b2_v[...]
    pre2[...] = summed
    act2, _ = gelu_parts(summed)

    arrived(land_recv, l_send, l_recv)
    flags_own = nn(pml, land_recv[...].reshape(lrows, 128).astype(BF16))
    flags_own = (flags_own * own_weight)[:slots].astype(BF16)

    def back(scaled, at, size, total):
        count_ = scaled.shape[0]
        hh, hl = head_hi[at:at + size, :], head_lo[at:at + size, :]
        high, low = halves(scaled)
        both = nn(jnp.concatenate([high, low], axis=0), hh)
        return total + both[:count_] + both[count_:] + nn(high, hl)

    terms = jnp.zeros((slots, hid), F32)
    for at, size in spans:
        span = slice(at, at + size)
        scaled = nn(flags_own, ok_rows[:, span]) * inv_row[:, span] * (value_v[:, span] - hb_v[span].reshape(1, size))
        terms = back(scaled, at, size, terms)
    high, low = halves(terms)
    both = jnp.concatenate([high, low], axis=1)
    if slots < 128:
        both = jnp.concatenate([both, jnp.zeros((128 - slots, 2 * hid), BF16)], axis=0)
    rows = n_lat * MSG
    upper = lax.rem(lax.broadcasted_iota(jnp.int32, (rows, 128), 0), MSG) < CAP
    sent_terms = nn(pmt[...], both)
    sent_terms = sent_terms[:, :hid] + sent_terms[:, hid:]
    term_send[...] = jnp.where(upper, sent_terms[:, :128], sent_terms[:, 128:]).reshape(n_lat, MSG, 128)
    terms_sent = exchange(term_send, term_recv, t_send, t_recv)

    high, low = halves(act2)
    cols = nn(oh[...], jnp.concatenate([high, low], axis=1)).astype(BF16)
    cols_hi, cols_lo = cols[:, :hid], cols[:, hid:]
    cols_both = jnp.concatenate([cols_hi, cols_lo], axis=0)
    terms = jnp.zeros((taken, hid), F32)
    for at, size in spans:
        span = slice(at, at + size)
        both = nt(cols_both, head_hi[span, :])
        decoded = both[:taken] + both[taken:] + nt(cols_hi, head_lo[span, :])
        terms = back(nn(flags_w, ok_rows[:, span]) * inv_row[:, span] * decoded, at, size, terms)

    wanted_row = jnp.transpose(jnp.broadcast_to(wanted.astype(F32), (taken, 128)))[0:1, :].astype(jnp.int32)
    oht[...] = jnp.where(wanted_row == lax.broadcasted_iota(jnp.int32, (512, taken), 0), 1.0, 0.0).astype(BF16)
    named = [jnp.sum(jnp.where(pick[a:a + 1] == msg_k, cellsf[a:a + 1], 0.0), axis=1, keepdims=True)
             for a in range(n_lat)]
    named = jnp.broadcast_to(jnp.concatenate(named, axis=0), (rows, 128))
    wanted_row = jnp.transpose(named)[0:1, :].astype(jnp.int32) - 1
    oht_msg[...] = jnp.where(wanted_row == lax.broadcasted_iota(jnp.int32, (512, rows), 0), 1.0, 0.0).astype(BF16)
    high, low = halves(terms)
    hidden = nn(oht[...], jnp.concatenate([high, low], axis=1))
    hidden = hidden[:, :hid] + hidden[:, hid:]
    pre2[...] = gelu_slope(pre2[...])
    pre1[...] = gelu_slope(pre1[...])
    for copy in rim1 + land_sent:
        copy.wait_send()

    arrived(term_recv, t_send, t_recv)

    came = term_recv[...].reshape(rows, 128)
    came = jnp.concatenate([jnp.where(upper, came, 0.0), jnp.where(upper, 0.0, came)], axis=1)
    high, low = halves(came)
    came = nn(oht_msg[...], jnp.concatenate([high, low], axis=1))
    grad2 = (hidden - came[:, :hid] - came[:, hid:]) * pre2[...]
    g_ext[2:10, SIDE:SIDE + 64, :] = grad2.reshape(8, 64, hid)
    rim2 = rim(g_ext, g_send, g_recv)
    for copy in terms_sent:
        copy.wait_send()

    rim_arrived(g_ext, g_recv, g_send)

    for j in range(3):
        span = slice(SIDE - j, SIDE - j + WIDE)

        def row(at, length=1):
            return g_ext[pl.ds(at, length), span, :]

        r0, r1, r10, r11 = row(north), row(1 - north), row(10 + south), row(11 - south)
        pieces = (
            (0, r0), (1, r1), (2, row(2, 8)), (10, r10), (11, r11),
            (12, row(2) + northf * r0), (13, row(3) + northf * r1),
            (14, r10 * (1.0 - southf)), (15, r11 * (1.0 - southf)),
            (16, r0 * (1.0 - northf)), (17, r1 * (1.0 - northf)),
            (18, row(8) + southf * r10), (19, row(9) + southf * r11),
        )
        for at, piece in pieces:
            high, low = halves(piece)
            sg_hi[j, at:at + piece.shape[0]] = high
            sg_lo[j, at:at + piece.shape[0]] = low

    def taps3(ref):
        parts = []
        for i in range(3):
            for j in range(3):
                if i == 0:
                    rows_ = jnp.concatenate([ref[j, 12:14], ref[j, 4:10], ref[j, 14:16]], axis=0)
                elif i == 1:
                    rows_ = ref[j, 1:11]
                else:
                    rows_ = jnp.concatenate([ref[j, 16:18], ref[j, 2:8], ref[j, 18:20]], axis=0)
                parts.append(rows_.reshape(10 * WIDE, hid))
        return jnp.concatenate(parts, axis=1)

    wh = jnp.concatenate([w2_hi[t * hid:(t + 1) * hid] for t in range(9)], axis=1)
    wl = jnp.concatenate([w2_lo[t * hid:(t + 1) * hid] for t in range(9)], axis=1)
    lhs = taps3(sg_hi)
    grad1 = nt(lhs, wh) + nt(lhs, wl) + nt(taps3(sg_lo), wh)
    p_ext[...] = grad1.reshape(10, WIDE, hid) * pre1[...]

    for j in range(3):
        span = slice(2 - j, 2 - j + 64)
        q0, q9 = p_ext[0:1, span, :], p_ext[9:10, span, :]
        pieces = (
            (0, p_ext[:, span, :]),
            (10, p_ext[2:3, span, :] + northf * q0), (11, q9 * (1.0 - southf)),
            (12, q0 * (1.0 - northf)), (13, p_ext[7:8, span, :] + southf * q9),
        )
        for at, piece in pieces:
            high, low = halves(piece)
            sp_hi[j, at:at + piece.shape[0]] = high
            sp_lo[j, at:at + piece.shape[0]] = low

    def taps4(ref):
        parts = []
        for i in range(3):
            for j in range(3):
                if i == 0:
                    rows_ = jnp.concatenate([ref[j, 10:11], ref[j, 3:9], ref[j, 11:12]], axis=0)
                elif i == 1:
                    rows_ = ref[j, 1:9]
                else:
                    rows_ = jnp.concatenate([ref[j, 12:13], ref[j, 1:7], ref[j, 13:14]], axis=0)
                parts.append(rows_.reshape(512, hid))
        return jnp.concatenate(parts, axis=1)

    wh = jnp.concatenate([w1_hi[t * k1:(t + 1) * k1] for t in range(9)], axis=1)
    wl = jnp.concatenate([w1_lo[t * k1:(t + 1) * k1] for t in range(9)], axis=1)
    both = nt(taps4(sp_hi), jnp.concatenate([wh, wl], axis=0))
    result = both[:, :k1] + both[:, k1:] + nt(taps4(sp_lo), wh)
    out_v[...] = result.reshape(8, 64, k1)
    done = pltpu.make_async_copy(out_v, out, load_sem.at[0])
    done.start()
    for copy in rim2:
        copy.wait_send()
    done.wait()


def shards(n_lon, n_lat, latent, conv1_weight, conv1_bias, conv2_weight, conv2_bias, head_weight, head_bias, land_sea,
           var_ok, obs_error, obs_band, obs_cell, obs_count, obs_value):
    lc, hid = conv1_weight.shape[2], conv1_weight.shape[3]
    slots, patch = obs_value.shape[1], obs_value.shape[2]
    variables = var_ok.shape[1]
    listed = n_lat * slots
    padded = -(-(listed + 128) // 128) * 128
    vmem = pltpu.VMEM
    rows = n_lat * MSG
    scratch = [
        vmem((12, BUF, lc), F32),
        vmem((3, 12, WIDE, lc), BF16), vmem((3, 12, WIDE, lc), BF16),
        vmem((9 * lc, hid), F32), vmem((9 * lc, hid), BF16), vmem((9 * lc, hid), BF16),
        vmem((9 * hid, hid), F32), vmem((9 * hid, hid), BF16), vmem((9 * hid, hid), BF16),
        vmem((1, hid), F32), vmem((1, hid), F32),
        vmem((10, WIDE, hid), F32), vmem((10, WIDE, hid), F32),
        vmem((3, 10, 64, hid), BF16), vmem((3, 10, 64, hid), BF16),
        vmem((512, hid), F32),
        vmem((patch, hid), F32), vmem((patch, hid), BF16), vmem((patch, hid), BF16),
        vmem((patch,), F32), vmem(land_sea.shape, jnp.int32), vmem(var_ok.shape, jnp.int32),
        vmem((1, variables), F32),
        vmem((1, padded), jnp.int32), vmem((1, padded), jnp.int32), vmem((1, padded), jnp.int32),
        vmem((slots, patch), F32), vmem((128, patch), BF16), vmem((1, patch), F32),
        vmem((n_lat * CAP, 512), BF16), vmem((512, n_lat * CAP), BF16), vmem((512, rows), BF16),
        vmem((rows, 128), BF16),
        vmem((n_lat, LCAP, 128), F32), vmem((n_lat, LCAP, 128), F32),
        vmem((n_lat, MSG, 128), F32), vmem((n_lat, MSG, 128), F32),
        vmem((12, BUF, hid), F32),
        vmem((3, 20, WIDE, hid), BF16), vmem((3, 20, WIDE, hid), BF16),
        vmem((10, WIDE, hid), F32),
        vmem((3, 14, 64, hid), BF16), vmem((3, 14, 64, hid), BF16),
        vmem((8, 64, lc), F32),
        pltpu.SemaphoreType.DMA((14,)),
        pltpu.SemaphoreType.DMA((8,)), pltpu.SemaphoreType.DMA((9,)),
        pltpu.SemaphoreType.DMA((8,)), pltpu.SemaphoreType.DMA((9,)),
    ] + [pltpu.SemaphoreType.DMA((n_lat,))] * 4
    return pl.pallas_call(
        functools.partial(kernel, n_lon, n_lat, slots, patch, variables),
        out_shape=jax.ShapeDtypeStruct(latent.shape, F32),
        in_specs=[pl.BlockSpec(memory_space=pl.ANY)] * 14,
        out_specs=pl.BlockSpec(memory_space=pl.ANY),
        scratch_shapes=scratch,
        compiler_params=pltpu.CompilerParams(
            collective_id=0, has_side_effects=True, vmem_limit_bytes=60 * 1024 * 1024),
    )(latent, conv1_weight.reshape(9 * lc, hid), conv1_bias.reshape(1, hid), conv2_weight.reshape(9 * hid, hid),
      conv2_bias.reshape(1, hid), head_weight.T, head_bias, land_sea, var_ok,
      obs_error.reshape(1, variables), obs_band.reshape(1, listed), obs_cell, obs_count, obs_value[0])


def solution(mesh):
    in_specs = (
        P("lat", "lon", None),
        P(),
        P(),
        P(),
        P(),
        P(),
        P(),
        P("lat", "lon"),
        P(),
        P(),
        P("lon", None, None),
        P("lon", None),
        P("lon", None),
        P("lon", "lat", None),
    )
    out_specs = P("lat", "lon", None)
    body = functools.partial(shards, mesh.shape["lon"], mesh.shape["lat"])
    return jax.shard_map(body, mesh=mesh, in_specs=in_specs, out_specs=out_specs, check_vma=False)
```

time: 62.6 us -> 51.8 us (0.83)
  Pallas kernels: 59.4 us -> 50 us
  local copies, waits for them, and re-layouts: 3.02 us -> 1.67 us
    pallas_call x1, Pallas kernels: 59.4 us -> 50 us  [shards(): pl.pallas_call(functools.partial(kernel, n_lon, n_lat, slots, patch, vari...]
    reshape x1 -> x0, local copies, waits for them, and re-layouts: 1.34 us -> none  [shards(): head_bias.reshape(1, patch)]
where the time goes in v1:
time: 51.8 us; the launch traced here: 51.7 us
  Pallas kernels  50 us (97%)
  local copies, waits for them, and re-layouts  1.67 us (3%)
    pallas_call x1, Pallas kernels, shards(): pl.pallas_call(functools.partial(kernel, n_lon, n_lat, slots, patch, vari...  50 us
    unnamed x1, local copies, waits for them, and re-layouts  1.67 us

profile of v1, /device:TPU:1, one launch (start us, length us, event | category | flops | bytes accessed | tf_op | source)
XLA Modules:
  0.0 51.7 jit_solution(9382118063584448175)
XLA Ops:
  0.0 50.0 %shard_map.136 = f32[8,64,128]{2,1,0:T(8,128)} custom-call(f32[8,64,128]{2,1,0:T(8,128)} %latent.1, f32[1152,256]{1,0:T(8,128)} %bitcast.11, f32[1,256]{1,0:T(1,128)} %bitcast.13, f32[2304,256]{1,0:T(8,128)} %bitcast.9, f32[1,256]{1,0:T(1,128)} %bitcast.14, f32[4416,256]{1,0:T(8,128)} %bitcast.8, f32[4416]{0:T(1024)} %hbias.1, s32[64,512]{1,0:T(8,128)} %land.1, ...), custom_call_target="tpu_custom_call" | custom-call | tf_op jit(solution)/shard_map/pallas_call | solution.py:497
  50.0 1.7 %copy.16 = f32[8,64,128]{2,1,0:T(8,128)} copy(f32[8,64,128]{2,1,0:T(8,128)} %shard_map.136) | data formatting | bytes 524288

commit v2 on v1

--- a/solution.py
+++ b/solution.py
@@ -13,7 +13,7 @@
 MSG = 2 * CAP
 LCAP = 16
 SIDE = 8
-WIDE = 80
+PAIRS = 40
 BUF = 88
 CHUNK = 512
 MESH = pl.DeviceIdType.MESH
@@ -50,7 +50,7 @@
     out,
     lat_ext, sa_hi, sa_lo, w1_v, w1_hi, w1_lo, w2_v, w2_hi, w2_lo, b1_v, b2_v,
     pre1, act1, sb_hi, sb_lo, pre2, head_v, head_hi, head_lo, hb_v, land_v, ok_v, err_v,
-    band_v, cell_v, count_v, value_v, ok_rows, inv_row,
+    band_v, cell_v, count_v, value_v, val_hi, val_lo, ok_rows, inv_row,
     oh, oht, oht_msg, pmt, land_send, land_recv, term_send, term_recv,
     g_ext, sg_hi, sg_lo, p_ext, sp_hi, sp_lo, out_v,
     load_sem, h_send, h_recv, g_send, g_recv, l_send, l_recv, t_send, t_recv,
@@ -60,14 +60,14 @@
     south = lax.div(lat + 1, n_lat)
     northf, southf = north.astype(F32), south.astype(F32)
     hid = w1_v.shape[1]
-    k1 = lat_ext.shape[2]
+    k1 = latent.shape[2]
 
     loads = [
         (band, band_v.at[:, 0:n_lat * slots]),
         (cell, cell_v.at[:, 0:n_lat * slots]),
         (count, count_v.at[:, 0:n_lat * slots]),
         (land, land_v),
-        (latent, lat_ext.at[2:10, SIDE:SIDE + 64, :]),
+        (latent, lat_ext.at[0, 2:10, SIDE:SIDE + 64, :]),
         (w1, w1_v),
         (b1, b1_v),
         (ok, ok_v),
@@ -123,8 +123,8 @@
             else:
                 dst_r, side = 2, 1
             slot = side * 3 + (1 - dc)
-            src = buf.at[pl.ds(src_r[0], src_r[1]), pl.ds(src_c[0], src_c[1]), :]
-            dst = buf.at[pl.ds(dst_r, src_r[1]), pl.ds(dst_c, src_c[1]), :]
+            src = buf.at[:, pl.ds(src_r[0], src_r[1]), pl.ds(src_c[0], src_c[1]), :]
+            dst = buf.at[:, pl.ds(dst_r, src_r[1]), pl.ds(dst_c, src_c[1]), :]
             copy = pltpu.make_async_remote_copy(
                 src_ref=src, dst_ref=dst, send_sem=send_sem.at[number], recv_sem=recv_sem.at[slot],
                 device_id=device, device_id_type=MESH)
@@ -132,11 +132,13 @@
             sent.append(copy)
         return sent
 
-    def rim_arrived(buf, recv_sem, send_sem):
+    def rim_arrived(buf, recv_sem, send_sem, sides):
         for number, (dr, dc, device) in enumerate(around):
+            if (dr == 0) != sides:
+                continue
             rows_ = (0, 2) if dr < 0 else (10, 2) if dr > 0 else (2, 8)
             cols_ = (0, SIDE) if dc < 0 else (72, SIDE) if dc > 0 else (SIDE, 64)
-            ref = buf.at[pl.ds(rows_[0], rows_[1]), pl.ds(cols_[0], cols_[1]), :]
+            ref = buf.at[:, pl.ds(rows_[0], rows_[1]), pl.ds(cols_[0], cols_[1]), :]
             slot = (dr + 1) * 3 + dc + 1
             pltpu.make_async_remote_copy(
                 src_ref=ref, dst_ref=ref, send_sem=send_sem.at[number], recv_sem=recv_sem.at[slot],
@@ -162,14 +164,60 @@
     def split(src, high_ref, low_ref, step):
         def body(i, carry):
             at = pl.ds(pl.multiple_of(i * step, step), step)
-            high, low = halves(src[at, :])
-            high_ref[at, :] = high
-            low_ref[at, :] = low
+            high_ref[at, :], low_ref[at, :] = halves(src[at, :])
             return carry
         lax.fori_loop(0, src.shape[0] // step, body, 0)
 
-    lat_ext[:, 80:88, :] = jnp.zeros((12, 8, k1), F32)
-    g_ext[:, 80:88, :] = jnp.zeros((12, 8, hid), F32)
+    def split_taps(src, high_ref, low_ref, depth, step):
+        for i in range(3):
+            def body(n, carry):
+                g0, g1, g2 = (src[pl.ds(pl.multiple_of((3 * i + j) * depth + n * step, step), step), :] for j in range(3))
+                outer, inner = 0.5 * (g0 + g2), 0.5 * g1
+                at = pl.ds(pl.multiple_of(i * depth + n * step, step), step)
+                for m, factor in enumerate((g0, outer + inner, outer - inner, g2)):
+                    high_ref[m, at, :], low_ref[m, at, :] = halves(factor)
+                return carry
+            lax.fori_loop(0, depth // step, body, 0)
+
+    def factors(d0, d1, d2, d3):
+        return d0 - d2, d1 + d2, d2 - d1, d1 - d3
+
+    def pair_rows(buf, at, length=1):
+        def column(d):
+            lanes = [buf[h, pl.ds(at, length), pl.ds(SIDE - 2 + d, PAIRS, stride=2), :] for h in range(buf.shape[0])]
+            return jnp.concatenate(lanes, axis=2)
+        return factors(*[column(d) for d in range(4)])
+
+    def put_rows(high_ref, low_ref, at, pieces):
+        for m, piece in enumerate(pieces):
+            count_ = piece.shape[0] // 2
+            high_ref[m, at:at + count_], low_ref[m, at:at + count_] = halves(
+                piece.reshape(count_, 2 * PAIRS, piece.shape[2]))
+
+    def joined(*rows_):
+        return [jnp.concatenate(list(x), axis=0) for x in zip(*rows_)]
+
+    def inner_rows(buf, high_ref, low_ref):
+        pieces = pair_rows(buf, 2, 8)
+        put_rows(high_ref, low_ref, 0, pieces)
+        put_rows(high_ref, low_ref, 4, [x[1:7] for x in pieces])
+
+    def pair_sums(taken_hi, taken_lo, weights):
+        parts = []
+        for m in range(4):
+            lhs, (wh, wl, dot) = taken_hi(m), weights(m)
+            parts.append(dot(lhs, wh) + dot(lhs, wl) + dot(taken_lo(m), wh))
+        m0, m1, m2, m3 = parts
+        return m0 + m1 + m2, m1 - m2 - m3
+
+    def taps(ref, chosen):
+        def lhs(m):
+            rows_ = [jnp.concatenate([ref[m, a:b] for a, b in part], axis=0) for part in chosen]
+            return jnp.concatenate([x.reshape(x.shape[0] * x.shape[1], x.shape[2]) for x in rows_], axis=1)
+        return lhs
+
+    lat_ext[:, :, 80:88, :] = jnp.zeros((k1 // 128, 12, 8, 128), F32)
+    g_ext[:, :, 80:88, :] = jnp.zeros((hid // 128, 12, 8, 128), F32)
 
     ld_band.wait()
     ld_cell.wait()
@@ -186,6 +234,7 @@
     below = below.astype(F32).astype(BF16)
     mine = jnp.where(live & (bands == lat), 1.0, 0.0)
     pick = jnp.where(mine > 0.0, nn(mine.astype(BF16), below), -1.0)
+    cells = ((cells >> 6) << 5) + ((cells & 63) >> 1) + ((cells & 1) << 8)
     cellsf = cells.astype(F32) + 1.0
     countsf = counts.astype(F32) * 0.125
     msg_k = lax.rem(lax.broadcasted_iota(jnp.int32, (MSG, 128), 0), CAP).astype(F32)
@@ -203,7 +252,9 @@
     oh[...] = jnp.where(wanted == lax.broadcasted_iota(jnp.int32, (taken, 512), 1), 1.0, 0.0).astype(BF16)
 
     ld_land.wait()
-    fold = (lax.broadcasted_iota(jnp.int32, (64, 512), 1) >> 3) == lax.broadcasted_iota(jnp.int32, (64, 512), 0)
+    column = lax.broadcasted_iota(jnp.int32, (64, 512), 0)
+    column = ((column & 31) << 1) + (column >> 5)
+    fold = (lax.broadcasted_iota(jnp.int32, (64, 512), 1) >> 3) == column
     fold = jnp.where(fold, 1.0, 0.0).astype(BF16)
     kept = (lax.broadcasted_iota(jnp.int32, (8, 512), 1) & 7) == lax.broadcasted_iota(jnp.int32, (8, 512), 0)
     tiles = []
@@ -211,7 +262,7 @@
         strip = land_v[8 * r:8 * r + 8, :].astype(F32)
         spread = jnp.concatenate([jnp.where(kept, strip[p:p + 1], 0.0) for p in range(8)], axis=0)
         tiles.append(nt(fold, spread.astype(BF16)))
-    tiles = jnp.concatenate(tiles, axis=0)
+    tiles = jnp.concatenate([x[:32] for x in tiles] + [x[32:] for x in tiles], axis=0)
     tiles = jnp.concatenate([tiles, 1.0 - tiles], axis=1).astype(BF16)
     flags = nn(oh[...], tiles)
     lrows = n_lat * LCAP
@@ -227,7 +278,7 @@
     rim1 = rim(lat_ext, h_send, h_recv)
 
     ld_w1.wait()
-    split(w1_v, w1_hi, w1_lo, 128)
+    split_taps(w1_v, w1_hi, w1_lo, k1, 64)
 
     own = lax.broadcasted_iota(jnp.int32, (n_lat, 128), 0) == lat
     own_band = jnp.sum(jnp.where(own, bands, 0), axis=0, keepdims=True)
@@ -245,7 +296,7 @@
     ld_err.wait()
     ld_hb.wait()
     ld_w2.wait()
-    split(w2_v, w2_hi, w2_lo, 128)
+    split_taps(w2_v, w2_hi, w2_lo, hid, 64)
     inv = 1.0 / (err_v[...] * err_v[...])
     inv_hi = inv.astype(BF16).astype(F32)
     inv_mid = (inv - inv_hi).astype(BF16).astype(F32)
@@ -269,68 +320,54 @@
     ld_b1.wait()
     ld_b2.wait()
     ld_value.wait()
+    for at, size in spans:
+        span = slice(at, at + size)
+        shifted = (value_v[:, span] - hb_v[span].reshape(1, size)) * inv_row[:, span]
+        val_hi[:, span], val_lo[:, span] = halves(shifted)
     ld_head.wait()
     split(head_v, head_hi, head_lo, 96)
 
-    rim_arrived(lat_ext, h_recv, h_send)
-
-    for j in range(3):
-        span = slice(SIDE - 2 + j, SIDE - 2 + j + WIDE)
-        for at, source, length in ((0, north, 1), (1, 1 - north, 1), (2, 2, 8), (10, 10 + south, 1), (11, 11 - south, 1)):
-            high, low = halves(lat_ext[pl.ds(source, length), span, :])
-            sa_hi[j, at:at + length] = high
-            sa_lo[j, at:at + length] = low
-
-    def taps1(ref):
-        parts = []
-        for i in range(3):
-            for j in range(3):
-                if i == 1:
-                    rows_ = ref[j, 1:11]
-                else:
-                    first = 2 * north if i == 0 else 2 - 2 * north
-                    last = 9 + 2 * south if i == 0 else 11 - 2 * south
-                    rows_ = jnp.concatenate(
-                        [ref[j, pl.ds(first, 1)], ref[j, 1 + i:9 + i], ref[j, pl.ds(last, 1)]], axis=0)
-                parts.append(rows_.reshape(10 * WIDE, rows_.shape[2]))
-        return jnp.concatenate(parts, axis=1)
-
-    wh, wl = w1_hi[...], w1_lo[...]
-    lhs = taps1(sa_hi)
-    summed = nn(lhs, wh) + nn(lhs, wl) + nn(taps1(sa_lo), wh) + b1_v[...]
-    pre1[...] = summed.reshape(10, WIDE, hid)
-    act1[...] = gelu_parts(summed)[0].reshape(10, WIDE, hid)
-
-    for j in range(3):
-        high, low = halves(act1[:, j:j + 64, :])
-        sb_hi[j] = high
-        sb_lo[j] = low
-
-    def taps2(ref):
-        return jnp.concatenate([ref[j, i:i + 8].reshape(512, hid) for i in range(3) for j in range(3)], axis=1)
-
-    wh, wl = w2_hi[...], w2_lo[...]
-    lhs = taps2(sb_hi)
-    summed = nn(lhs, wh) + nn(lhs, wl) + nn(taps2(sb_lo), wh) + b2_v[...]
-    pre2[...] = summed
-    act2, _ = gelu_parts(summed)
+    rim_arrived(lat_ext, h_recv, h_send, True)
+
+    def forward1(m):
+        return w1_hi[m], w1_lo[m], nn
+
+    def put1(chosen, groups):
+        for parity, summed in enumerate(pair_sums(taps(sa_hi, chosen), taps(sa_lo, chosen), forward1)):
+            summed = summed + b1_v[...]
+            act = gelu_parts(summed)[0]
+            for source, target, length in groups:
+                part = slice(source * PAIRS, (source + length) * PAIRS)
+                pre1[parity, target:target + length] = summed[part].reshape(length, PAIRS, hid)
+                act1[parity, target:target + length] = act[part].reshape(length, PAIRS, hid)
+
+    inner_rows(lat_ext, sa_hi, sa_lo)
+    put1((((0, 3),), ((4, 7),), ((1, 4),)), ((0, 2, 6),))
+    rim_arrived(lat_ext, h_recv, h_send, False)
+    for at, one, other in (
+        (7, 1 - north, 2), (8, 9, 10 + south),
+        (9, 2 * north, 1 - north), (10, 8, 9 + south),
+        (11, 2 - north, 3), (12, 10 + south, 11 - 2 * south),
+    ):
+        put_rows(sa_hi, sa_lo, at, joined(pair_rows(lat_ext, one), pair_rows(lat_ext, other)))
+    put1((((9, 11),), ((7, 9),), ((11, 13),)), ((0, 0, 2), (2, 8, 2)))
 
     arrived(land_recv, l_send, l_recv)
     flags_own = nn(pml, land_recv[...].reshape(lrows, 128).astype(BF16))
-    flags_own = (flags_own * own_weight)[:slots].astype(BF16)
-
-    def back(scaled, at, size, total):
-        count_ = scaled.shape[0]
+    flags_own = flags_own[:slots].astype(BF16)
+
+    def back(high, low, at, size, total):
+        count_ = high.shape[0]
         hh, hl = head_hi[at:at + size, :], head_lo[at:at + size, :]
-        high, low = halves(scaled)
         both = nn(jnp.concatenate([high, low], axis=0), hh)
         return total + both[:count_] + both[count_:] + nn(high, hl)
 
     terms = jnp.zeros((slots, hid), F32)
     for at, size in spans:
         span = slice(at, at + size)
-        scaled = nn(flags_own, ok_rows[:, span]) * inv_row[:, span] * (value_v[:, span] - hb_v[span].reshape(1, size))
-        terms = back(scaled, at, size, terms)
+        seen = nn(flags_own, ok_rows[:, span]).astype(BF16)
+        terms = back(val_hi[:, span] * seen, val_lo[:, span] * seen, at, size, terms)
+    terms = terms * own_weight[:slots]
     high, low = halves(terms)
     both = jnp.concatenate([high, low], axis=1)
     if slots < 128:
@@ -342,6 +379,20 @@
     term_send[...] = jnp.where(upper, sent_terms[:, :128], sent_terms[:, 128:]).reshape(n_lat, MSG, 128)
     terms_sent = exchange(term_send, term_recv, t_send, t_recv)
 
+    def near(ref, rows_=slice(0, 10)):
+        return factors(ref[0, rows_, 0:32], ref[1, rows_, 0:32], ref[0, rows_, 1:33], ref[1, rows_, 1:33])
+
+    for m, piece in enumerate(near(act1)):
+        sb_hi[m], sb_lo[m] = halves(piece)
+
+    def forward2(m):
+        return w2_hi[m], w2_lo[m], nn
+
+    chosen = tuple(((i, i + 8),) for i in range(3))
+    summed = jnp.concatenate(pair_sums(taps(sb_hi, chosen), taps(sb_lo, chosen), forward2), axis=0) + b2_v[...]
+    pre2[...] = summed
+    act2, _ = gelu_parts(summed)
+
     high, low = halves(act2)
     cols = nn(oh[...], jnp.concatenate([high, low], axis=1)).astype(BF16)
     cols_hi, cols_lo = cols[:, :hid], cols[:, hid:]
@@ -351,7 +402,8 @@
         span = slice(at, at + size)
         both = nt(cols_both, head_hi[span, :])
         decoded = both[:taken] + both[taken:] + nt(cols_hi, head_lo[span, :])
-        terms = back(nn(flags_w, ok_rows[:, span]) * inv_row[:, span] * decoded, at, size, terms)
+        high, low = halves(nn(flags_w, ok_rows[:, span]) * inv_row[:, span] * decoded)
+        terms = back(high, low, at, size, terms)
 
     wanted_row = jnp.transpose(jnp.broadcast_to(wanted.astype(F32), (taken, 128)))[0:1, :].astype(jnp.int32)
     oht[...] = jnp.where(wanted_row == lax.broadcasted_iota(jnp.int32, (512, taken), 0), 1.0, 0.0).astype(BF16)
@@ -375,82 +427,67 @@
     high, low = halves(came)
     came = nn(oht_msg[...], jnp.concatenate([high, low], axis=1))
     grad2 = (hidden - came[:, :hid] - came[:, hid:]) * pre2[...]
-    g_ext[2:10, SIDE:SIDE + 64, :] = grad2.reshape(8, 64, hid)
+    for parity in range(2):
+        for h in range(hid // 128):
+            part = grad2[256 * parity:256 * parity + 256, 128 * h:128 * h + 128]
+            g_ext[h, 2:10, pl.ds(SIDE + parity, 32, stride=2), :] = part.reshape(8, 32, 128)
     rim2 = rim(g_ext, g_send, g_recv)
     for copy in terms_sent:
         copy.wait_send()
 
-    rim_arrived(g_ext, g_recv, g_send)
-
-    for j in range(3):
-        span = slice(SIDE - j, SIDE - j + WIDE)
-
-        def row(at, length=1):
-            return g_ext[pl.ds(at, length), span, :]
-
-        r0, r1, r10, r11 = row(north), row(1 - north), row(10 + south), row(11 - south)
-        pieces = (
-            (0, r0), (1, r1), (2, row(2, 8)), (10, r10), (11, r11),
-            (12, row(2) + northf * r0), (13, row(3) + northf * r1),
-            (14, r10 * (1.0 - southf)), (15, r11 * (1.0 - southf)),
-            (16, r0 * (1.0 - northf)), (17, r1 * (1.0 - northf)),
-            (18, row(8) + southf * r10), (19, row(9) + southf * r11),
-        )
-        for at, piece in pieces:
-            high, low = halves(piece)
-            sg_hi[j, at:at + piece.shape[0]] = high
-            sg_lo[j, at:at + piece.shape[0]] = low
-
-    def taps3(ref):
-        parts = []
-        for i in range(3):
-            for j in range(3):
-                if i == 0:
-                    rows_ = jnp.concatenate([ref[j, 12:14], ref[j, 4:10], ref[j, 14:16]], axis=0)
-                elif i == 1:
-                    rows_ = ref[j, 1:11]
-                else:
-                    rows_ = jnp.concatenate([ref[j, 16:18], ref[j, 2:8], ref[j, 18:20]], axis=0)
-                parts.append(rows_.reshape(10 * WIDE, hid))
-        return jnp.concatenate(parts, axis=1)
-
-    wh = jnp.concatenate([w2_hi[t * hid:(t + 1) * hid] for t in range(9)], axis=1)
-    wl = jnp.concatenate([w2_lo[t * hid:(t + 1) * hid] for t in range(9)], axis=1)
-    lhs = taps3(sg_hi)
-    grad1 = nt(lhs, wh) + nt(lhs, wl) + nt(taps3(sg_lo), wh)
-    p_ext[...] = grad1.reshape(10, WIDE, hid) * pre1[...]
-
-    for j in range(3):
-        span = slice(2 - j, 2 - j + 64)
-        q0, q9 = p_ext[0:1, span, :], p_ext[9:10, span, :]
-        pieces = (
-            (0, p_ext[:, span, :]),
-            (10, p_ext[2:3, span, :] + northf * q0), (11, q9 * (1.0 - southf)),
-            (12, q0 * (1.0 - northf)), (13, p_ext[7:8, span, :] + southf * q9),
-        )
-        for at, piece in pieces:
-            high, low = halves(piece)
-            sp_hi[j, at:at + piece.shape[0]] = high
-            sp_lo[j, at:at + piece.shape[0]] = low
-
-    def taps4(ref):
-        parts = []
-        for i in range(3):
-            for j in range(3):
-                if i == 0:
-                    rows_ = jnp.concatenate([ref[j, 10:11], ref[j, 3:9], ref[j, 11:12]], axis=0)
-                elif i == 1:
-                    rows_ = ref[j, 1:9]
-                else:
-                    rows_ = jnp.concatenate([ref[j, 12:13], ref[j, 1:7], ref[j, 13:14]], axis=0)
-                parts.append(rows_.reshape(512, hid))
-        return jnp.concatenate(parts, axis=1)
-
-    wh = jnp.concatenate([w1_hi[t * k1:(t + 1) * k1] for t in range(9)], axis=1)
-    wl = jnp.concatenate([w1_lo[t * k1:(t + 1) * k1] for t in range(9)], axis=1)
-    both = nt(taps4(sp_hi), jnp.concatenate([wh, wl], axis=0))
-    result = both[:, :k1] + both[:, k1:] + nt(taps4(sp_lo), wh)
-    out_v[...] = result.reshape(8, 64, k1)
+    rim_arrived(g_ext, g_recv, g_send, True)
+
+    def backward(high_ref, low_ref, depth):
+        def weights(m):
+            at = (3, 1, 2, 0)[m]
+            return tuple(jnp.concatenate([ref[at, i * depth:(i + 1) * depth] for i in range(3)], axis=1)
+                         for ref in (high_ref, low_ref)) + (nt,)
+        return weights
+
+    def put2(chosen, groups):
+        sums = pair_sums(taps(sg_hi, chosen), taps(sg_lo, chosen), backward(w2_hi, w2_lo, hid))
+        for parity, grad1 in enumerate(sums):
+            for source, target, length in groups:
+                part = grad1[source * PAIRS:(source + length) * PAIRS].reshape(length, PAIRS, hid)
+                p_ext[parity, target:target + length] = part * pre1[parity, target:target + length]
+
+    inner_rows(g_ext, sg_hi, sg_lo)
+    put2((((1, 4),), ((4, 7),), ((0, 3),)), ((0, 2, 6),))
+    rim_arrived(g_ext, g_recv, g_send, False)
+    r0, r1 = pair_rows(g_ext, north), pair_rows(g_ext, 1 - north)
+    r10, r11 = pair_rows(g_ext, 10 + south), pair_rows(g_ext, 11 - south)
+
+    def scaled_by(x, factor):
+        return [y * factor for y in x]
+
+    def plus(x, y, factor):
+        return [u + v * factor for u, v in zip(x, y)]
+
+    put_rows(sg_hi, sg_lo, 7, joined(r1, pair_rows(g_ext, 2)))
+    put_rows(sg_hi, sg_lo, 8, joined(pair_rows(g_ext, 9), r10))
+    put_rows(sg_hi, sg_lo, 9, joined(plus(pair_rows(g_ext, 2), r0, northf), plus(pair_rows(g_ext, 3), r1, northf)))
+    put_rows(sg_hi, sg_lo, 10, joined(scaled_by(r10, 1.0 - southf), scaled_by(r11, 1.0 - southf)))
+    put_rows(sg_hi, sg_lo, 11, joined(scaled_by(r0, 1.0 - northf), scaled_by(r1, 1.0 - northf)))
+    put_rows(sg_hi, sg_lo, 12, joined(plus(pair_rows(g_ext, 8), r10, southf), plus(pair_rows(g_ext, 9), r11, southf)))
+    put2((((9, 11),), ((7, 9),), ((11, 13),)), ((0, 0, 2), (2, 8, 2)))
+
+    for m, piece in enumerate(near(p_ext)):
+        q0, q9 = piece[0:1], piece[9:10]
+        for at, part in (
+            (0, piece), (10, piece[2:3] + northf * q0), (11, q9 * (1.0 - southf)),
+            (12, q0 * (1.0 - northf)), (13, piece[7:8] + southf * q9),
+        ):
+            sp_hi[m, at:at + part.shape[0]], sp_lo[m, at:at + part.shape[0]] = halves(part)
+
+    chosen = (((10, 11), (3, 9), (11, 12)), ((1, 9),), ((12, 13), (1, 7), (13, 14)))
+    parts = []
+    for m in range(4):
+        wh, wl, dot = backward(w1_hi, w1_lo, k1)(m)
+        both = dot(taps(sp_hi, chosen)(m), jnp.concatenate([wh, wl], axis=0))
+        parts.append(both[:, :k1] + both[:, k1:] + dot(taps(sp_lo, chosen)(m), wh))
+    m0, m1, m2, m3 = parts
+    for parity, part in enumerate((m0 + m1 + m2, m1 - m2 - m3)):
+        out_v[:, pl.ds(parity, 32, stride=2), :] = part.reshape(8, 32, k1)
     done = pltpu.make_async_copy(out_v, out, load_sem.at[0])
     done.start()
     for copy in rim2:
@@ -468,27 +505,28 @@
     vmem = pltpu.VMEM
     rows = n_lat * MSG
     scratch = [
-        vmem((12, BUF, lc), F32),
-        vmem((3, 12, WIDE, lc), BF16), vmem((3, 12, WIDE, lc), BF16),
-        vmem((9 * lc, hid), F32), vmem((9 * lc, hid), BF16), vmem((9 * lc, hid), BF16),
-        vmem((9 * hid, hid), F32), vmem((9 * hid, hid), BF16), vmem((9 * hid, hid), BF16),
+        vmem((lc // 128, 12, BUF, 128), F32),
+        vmem((4, 13, 2 * PAIRS, lc), BF16), vmem((4, 13, 2 * PAIRS, lc), BF16),
+        vmem((9 * lc, hid), F32), vmem((4, 3 * lc, hid), BF16), vmem((4, 3 * lc, hid), BF16),
+        vmem((9 * hid, hid), F32), vmem((4, 3 * hid, hid), BF16), vmem((4, 3 * hid, hid), BF16),
         vmem((1, hid), F32), vmem((1, hid), F32),
-        vmem((10, WIDE, hid), F32), vmem((10, WIDE, hid), F32),
-        vmem((3, 10, 64, hid), BF16), vmem((3, 10, 64, hid), BF16),
+        vmem((2, 10, PAIRS, hid), F32), vmem((2, 10, PAIRS, hid), F32),
+        vmem((4, 10, 32, hid), BF16), vmem((4, 10, 32, hid), BF16),
         vmem((512, hid), F32),
         vmem((patch, hid), F32), vmem((patch, hid), BF16), vmem((patch, hid), BF16),
         vmem((patch,), F32), vmem(land_sea.shape, jnp.int32), vmem(var_ok.shape, jnp.int32),
         vmem((1, variables), F32),
         vmem((1, padded), jnp.int32), vmem((1, padded), jnp.int32), vmem((1, padded), jnp.int32),
-        vmem((slots, patch), F32), vmem((128, patch), BF16), vmem((1, patch), F32),
+        vmem((slots, patch), F32), vmem((slots, patch), BF16), vmem((slots, patch), BF16),
+        vmem((128, patch), BF16), vmem((1, patch), F32),
         vmem((n_lat * CAP, 512), BF16), vmem((512, n_lat * CAP), BF16), vmem((512, rows), BF16),
         vmem((rows, 128), BF16),
         vmem((n_lat, LCAP, 128), F32), vmem((n_lat, LCAP, 128), F32),
         vmem((n_lat, MSG, 128), F32), vmem((n_lat, MSG, 128), F32),
-        vmem((12, BUF, hid), F32),
-        vmem((3, 20, WIDE, hid), BF16), vmem((3, 20, WIDE, hid), BF16),
-        vmem((10, WIDE, hid), F32),
-        vmem((3, 14, 64, hid), BF16), vmem((3, 14, 64, hid), BF16),
+        vmem((hid // 128, 12, BUF, 128), F32),
+        vmem((4, 13, 2 * PAIRS, hid), BF16), vmem((4, 13, 2 * PAIRS, hid), BF16),
+        vmem((2, 10, PAIRS, hid), F32),
+        vmem((4, 14, 32, hid), BF16), vmem((4, 14, 32, hid), BF16),
         vmem((8, 64, lc), F32),
         pltpu.SemaphoreType.DMA((14,)),
         pltpu.SemaphoreType.DMA((8,)), pltpu.SemaphoreType.DMA((9,)),

time: 51.8 us -> 42.2 us (0.81)
  Pallas kernels: 50 us -> 40.5 us
    pallas_call x1, Pallas kernels: 50 us -> 40.5 us  [shards(): pl.pallas_call(functools.partial(kernel, n_lon, n_lat, slots, patch, vari...]
where the time goes in v2:
time: 42.2 us; the launch traced here: 42.1 us
  Pallas kernels  40.5 us (96%)
  local copies, waits for them, and re-layouts  1.67 us (4%)
    pallas_call x1, Pallas kernels, shards(): pl.pallas_call(functools.partial(kernel, n_lon, n_lat, slots, patch, vari...  40.5 us
    unnamed x1, local copies, waits for them, and re-layouts  1.67 us

profile of v2, /device:TPU:1, one launch (start us, length us, event | category | flops | bytes accessed | tf_op | source)
XLA Modules:
  0.0 42.1 jit_solution(6524770590205035895)
XLA Ops:
  0.0 40.5 %shard_map.136 = f32[8,64,128]{2,1,0:T(8,128)} custom-call(f32[8,64,128]{2,1,0:T(8,128)} %latent.1, f32[1152,256]{1,0:T(8,128)} %bitcast.11, f32[1,256]{1,0:T(1,128)} %bitcast.13, f32[2304,256]{1,0:T(8,128)} %bitcast.9, f32[1,256]{1,0:T(1,128)} %bitcast.14, f32[4416,256]{1,0:T(8,128)} %bitcast.8, f32[4416]{0:T(1024)} %hbias.1, s32[64,512]{1,0:T(8,128)} %land.1, ...), custom_call_target="tpu_custom_call" | custom-call | tf_op jit(solution)/shard_map/pallas_call | solution.py:535
  40.5 1.7 %copy.16 = f32[8,64,128]{2,1,0:T(8,128)} copy(f32[8,64,128]{2,1,0:T(8,128)} %shard_map.136) | data formatting | bytes 524288

commit v3 on v2

--- a/solution.py
+++ b/solution.py
@@ -50,9 +50,9 @@
     out,
     lat_ext, sa_hi, sa_lo, w1_v, w1_hi, w1_lo, w2_v, w2_hi, w2_lo, b1_v, b2_v,
     pre1, act1, sb_hi, sb_lo, pre2, head_v, head_hi, head_lo, hb_v, land_v, ok_v, err_v,
-    band_v, cell_v, count_v, value_v, val_hi, val_lo, ok_rows, inv_row,
-    oh, oht, oht_msg, pmt, land_send, land_recv, term_send, term_recv,
-    g_ext, sg_hi, sg_lo, p_ext, sp_hi, sp_lo, out_v,
+    band_v, cell_v, count_v, value_v, val_hi, val_lo, masked, ok_rows, inv_row,
+    oh, oht, oht_msg, pmt, from_land, own_weight, land_send, land_recv, term_send, term_recv,
+    g_ext, sg_hi, sg_lo, p_ext, sp_hi, sp_lo,
     load_sem, h_send, h_recv, g_send, g_recv, l_send, l_recv, t_send, t_recv,
 ):
     lon, lat = lax.axis_index("lon"), lax.axis_index("lat")
@@ -110,36 +110,60 @@
     for copy in copies[5:]:
         copy.start()
 
-    def rim(buf, send_sem, recv_sem):
+    near_rows, far_rows, corners, sides = range(4)
+    parts = []
+    for dr, dc, device in around:
+        if dr and not dc:
+            parts += [(near_rows, dr, dc, device), (far_rows, dr, dc, device)]
+        else:
+            parts.append((corners if dr else sides, dr, dc, device))
+
+    def rim(buf, send_sem, recv_sem, kinds):
         sent = []
-        for number, (dr, dc, device) in enumerate(around):
-            src_r = (2, 2) if dr < 0 else (8, 2) if dr > 0 else (2, 8)
-            src_c = (SIDE, SIDE) if dc < 0 else (SIDE + 56, SIDE) if dc > 0 else (SIDE, 64)
-            dst_c = 72 if dc < 0 else 0 if dc > 0 else SIDE
-            if dr < 0:
-                dst_r, side = 10 - 10 * north, 2 - 2 * north
-            elif dr > 0:
-                dst_r, side = 10 * south, 2 * south
+        for kind in kinds:
+            for number, (its, dr, dc, device) in enumerate(parts):
+                if its != kind:
+                    continue
+                src_c = (SIDE, SIDE) if dc < 0 else (SIDE + 56, SIDE) if dc > 0 else (SIDE, 64)
+                dst_c = 72 if dc < 0 else 0 if dc > 0 else SIDE
+                second = 1 if kind == far_rows else 0
+                if dr < 0:
+                    src_r, dst_r, side = 2 + second, 10 - 10 * north + second, 2 - 2 * north
+                elif dr > 0:
+                    src_r, dst_r, side = 9 - second, 1 + 10 * south - second, 2 * south
+                else:
+                    src_r, dst_r, side = 2, 2, 1
+                length = 8 if kind == sides else 1
+                if kind == corners:
+                    length = 2
+                    if dr > 0:
+                        src_r, dst_r = 8, 10 * south
+                slot = 9 * second + side * 3 + (1 - dc)
+                src = buf.at[:, pl.ds(src_r, length), pl.ds(src_c[0], src_c[1]), :]
+                dst = buf.at[:, pl.ds(dst_r, length), pl.ds(dst_c, src_c[1]), :]
+                copy = pltpu.make_async_remote_copy(
+                    src_ref=src, dst_ref=dst, send_sem=send_sem.at[number], recv_sem=recv_sem.at[slot],
+                    device_id=device, device_id_type=MESH)
+                copy.start()
+                sent.append(copy)
+        return sent
+
+    def rim_arrived(buf, recv_sem, send_sem, kinds):
+        for number, (kind, dr, dc, device) in enumerate(parts):
+            if kind not in kinds:
+                continue
+            cols_ = (0, SIDE) if dc < 0 else (72, SIDE) if dc > 0 else (SIDE, 64)
+            second = 1 if kind == far_rows else 0
+            if kind == sides:
+                at, length = 2, 8
+            elif kind == corners:
+                at, length = (0 if dr < 0 else 10), 2
             else:
-                dst_r, side = 2, 1
-            slot = side * 3 + (1 - dc)
-            src = buf.at[:, pl.ds(src_r[0], src_r[1]), pl.ds(src_c[0], src_c[1]), :]
-            dst = buf.at[:, pl.ds(dst_r, src_r[1]), pl.ds(dst_c, src_c[1]), :]
-            copy = pltpu.make_async_remote_copy(
-                src_ref=src, dst_ref=dst, send_sem=send_sem.at[number], recv_sem=recv_sem.at[slot],
-                device_id=device, device_id_type=MESH)
-            copy.start()
-            sent.append(copy)
-        return sent
-
-    def rim_arrived(buf, recv_sem, send_sem, sides):
-        for number, (dr, dc, device) in enumerate(around):
-            if (dr == 0) != sides:
-                continue
-            rows_ = (0, 2) if dr < 0 else (10, 2) if dr > 0 else (2, 8)
-            cols_ = (0, SIDE) if dc < 0 else (72, SIDE) if dc > 0 else (SIDE, 64)
-            ref = buf.at[:, pl.ds(rows_[0], rows_[1]), pl.ds(cols_[0], cols_[1]), :]
-            slot = (dr + 1) * 3 + dc + 1
+                at, length = (1 - north if dr < 0 else 10 + south), 1
+                if second:
+                    at = north if dr < 0 else 11 - south
+            ref = buf.at[:, pl.ds(at, length), pl.ds(cols_[0], cols_[1]), :]
+            slot = 9 * second + (dr + 1) * 3 + dc + 1
             pltpu.make_async_remote_copy(
                 src_ref=ref, dst_ref=ref, send_sem=send_sem.at[number], recv_sem=recv_sem.at[slot],
                 device_id=device, device_id_type=MESH).wait_recv()
@@ -203,11 +227,11 @@
         put_rows(high_ref, low_ref, 4, [x[1:7] for x in pieces])
 
     def pair_sums(taken_hi, taken_lo, weights):
-        parts = []
+        products = []
         for m in range(4):
             lhs, (wh, wl, dot) = taken_hi(m), weights(m)
-            parts.append(dot(lhs, wh) + dot(lhs, wl) + dot(taken_lo(m), wh))
-        m0, m1, m2, m3 = parts
+            products.append(dot(lhs, wh) + dot(lhs, wl) + dot(taken_lo(m), wh))
+        m0, m1, m2, m3 = products
         return m0 + m1 + m2, m1 - m2 - m3
 
     def taps(ref, chosen):
@@ -275,7 +299,7 @@
     pl.semaphore_wait(barrier, len(around) + len(peers))
     land_sent = exchange(land_send, land_recv, l_send, l_recv)
     ld_lat.wait()
-    rim1 = rim(lat_ext, h_send, h_recv)
+    rim1 = rim(lat_ext, h_send, h_recv, (sides, near_rows, corners, far_rows))
 
     ld_w1.wait()
     split_taps(w1_v, w1_hi, w1_lo, k1, 64)
@@ -289,8 +313,8 @@
     pmt[...] = jnp.concatenate(
         [jnp.where(place[b:b + 1] == msg_k, 1.0, 0.0) for b in range(n_lat)], axis=0).astype(BF16)
     pml = jnp.concatenate([jnp.where(place[b:b + 1] == land_k, 1.0, 0.0) for b in range(n_lat)], axis=0)
-    pml = jnp.transpose(pml).astype(BF16)
-    own_weight = jnp.transpose(jnp.broadcast_to(own_count, (128, 128)))[:, 0:1]
+    from_land[...] = jnp.transpose(pml).astype(BF16)
+    own_weight[...] = jnp.transpose(jnp.broadcast_to(own_count, (128, 128)))
 
     ld_ok.wait()
     ld_err.wait()
@@ -327,7 +351,7 @@
     ld_head.wait()
     split(head_v, head_hi, head_lo, 96)
 
-    rim_arrived(lat_ext, h_recv, h_send, True)
+    rim_arrived(lat_ext, h_recv, h_send, (sides,))
 
     def forward1(m):
         return w1_hi[m], w1_lo[m], nn
@@ -343,7 +367,7 @@
 
     inner_rows(lat_ext, sa_hi, sa_lo)
     put1((((0, 3),), ((4, 7),), ((1, 4),)), ((0, 2, 6),))
-    rim_arrived(lat_ext, h_recv, h_send, False)
+    rim_arrived(lat_ext, h_recv, h_send, (near_rows, corners, far_rows))
     for at, one, other in (
         (7, 1 - north, 2), (8, 9, 10 + south),
         (9, 2 * north, 1 - north), (10, 8, 9 + south),
@@ -353,7 +377,7 @@
     put1((((9, 11),), ((7, 9),), ((11, 13),)), ((0, 0, 2), (2, 8, 2)))
 
     arrived(land_recv, l_send, l_recv)
-    flags_own = nn(pml, land_recv[...].reshape(lrows, 128).astype(BF16))
+    flags_own = nn(from_land[...], land_recv[...].reshape(lrows, 128).astype(BF16))
     flags_own = flags_own[:slots].astype(BF16)
 
     def back(high, low, at, size, total):
@@ -362,12 +386,17 @@
         both = nn(jnp.concatenate([high, low], axis=0), hh)
         return total + both[:count_] + both[count_:] + nn(high, hl)
 
-    terms = jnp.zeros((slots, hid), F32)
     for at, size in spans:
         span = slice(at, at + size)
         seen = nn(flags_own, ok_rows[:, span]).astype(BF16)
-        terms = back(val_hi[:, span] * seen, val_lo[:, span] * seen, at, size, terms)
-    terms = terms * own_weight[:slots]
+        masked[0:slots, span] = val_hi[:, span] * seen
+        masked[slots:2 * slots, span] = val_lo[:, span] * seen
+    cut = patch // 256 * 128
+    shares = jnp.concatenate([own_weight[0:slots, :]] * (hid // 128), axis=1)
+    terms = jnp.zeros((slots, hid), F32)
+    for a, b in ((0, cut), (cut, patch)):
+        both = nn(masked[:, a:b], head_hi[a:b, :])
+        terms = terms + (both[:slots] + both[slots:] + nn(masked[0:slots, a:b], head_lo[a:b, :])) * shares
     high, low = halves(terms)
     both = jnp.concatenate([high, low], axis=1)
     if slots < 128:
@@ -425,17 +454,26 @@
     came = term_recv[...].reshape(rows, 128)
     came = jnp.concatenate([jnp.where(upper, came, 0.0), jnp.where(upper, 0.0, came)], axis=1)
     high, low = halves(came)
-    came = nn(oht_msg[...], jnp.concatenate([high, low], axis=1))
-    grad2 = (hidden - came[:, :hid] - came[:, hid:]) * pre2[...]
-    for parity in range(2):
-        for h in range(hid // 128):
-            part = grad2[256 * parity:256 * parity + 256, 128 * h:128 * h + 128]
-            g_ext[h, 2:10, pl.ds(SIDE + parity, 32, stride=2), :] = part.reshape(8, 32, 128)
-    rim2 = rim(g_ext, g_send, g_recv)
+    came = jnp.concatenate([high, low], axis=1)
+
+    def put_grad(groups):
+        for first_, last in groups:
+            for parity in range(2):
+                cells_ = slice(256 * parity + 32 * first_, 256 * parity + 32 * last)
+                moved = nn(oht_msg[cells_, :], came)
+                grad2 = (hidden[cells_] - moved[:, :hid] - moved[:, hid:]) * pre2[cells_, :]
+                for h in range(hid // 128):
+                    g_ext[h, 2 + first_:2 + last, pl.ds(SIDE + parity, 32, stride=2), :] = (
+                        grad2[:, 128 * h:128 * h + 128].reshape(last - first_, 32, 128))
+
+    put_grad(((0, 2), (6, 8)))
+    rim2 = rim(g_ext, g_send, g_recv, (near_rows, corners, far_rows))
+    put_grad(((2, 6),))
+    rim2 += rim(g_ext, g_send, g_recv, (sides,))
     for copy in terms_sent:
         copy.wait_send()
 
-    rim_arrived(g_ext, g_recv, g_send, True)
+    rim_arrived(g_ext, g_recv, g_send, (sides,))
 
     def backward(high_ref, low_ref, depth):
         def weights(m):
@@ -451,18 +489,41 @@
                 part = grad1[source * PAIRS:(source + length) * PAIRS].reshape(length, PAIRS, hid)
                 p_ext[parity, target:target + length] = part * pre1[parity, target:target + length]
 
+    def scaled_by(x, factor):
+        return [y * factor for y in x]
+
+    def plus(x, y, factor):
+        return [u + v * factor for u, v in zip(x, y)]
+
+    def near_pairs(first_, last):
+        rows_ = slice(first_, last)
+        return factors(p_ext[0, rows_, 0:32], p_ext[1, rows_, 0:32], p_ext[0, rows_, 1:33], p_ext[1, rows_, 1:33])
+
+    def put_pairs(first_, last, at):
+        for m, piece in enumerate(near_pairs(first_, last)):
+            sp_hi[m, at:at + last - first_], sp_lo[m, at:at + last - first_] = halves(piece)
+
+    def put3(chosen, rows_):
+        products = []
+        for m in range(4):
+            wh, wl, dot = backward(w1_hi, w1_lo, k1)(m)
+            both_ = dot(taps(sp_hi, chosen)(m), jnp.concatenate([wh, wl], axis=0))
+            products.append(both_[:, :k1] + both_[:, k1:] + dot(taps(sp_lo, chosen)(m), wh))
+        m0, m1, m2, m3 = products
+        for parity, part in enumerate((m0 + m1 + m2, m1 - m2 - m3)):
+            part = part.reshape(part.shape[0] // 32, 32, k1)
+            done = 0
+            for first_, last in rows_:
+                out[first_:last, pl.ds(parity, 32, stride=2), :] = part[done:done + last - first_]
+                done += last - first_
+
     inner_rows(g_ext, sg_hi, sg_lo)
     put2((((1, 4),), ((4, 7),), ((0, 3),)), ((0, 2, 6),))
-    rim_arrived(g_ext, g_recv, g_send, False)
+    put_pairs(2, 8, 2)
+    put3((((4, 8),), ((3, 7),), ((2, 6),)), ((2, 6),))
+    rim_arrived(g_ext, g_recv, g_send, (near_rows, corners, far_rows))
     r0, r1 = pair_rows(g_ext, north), pair_rows(g_ext, 1 - north)
     r10, r11 = pair_rows(g_ext, 10 + south), pair_rows(g_ext, 11 - south)
-
-    def scaled_by(x, factor):
-        return [y * factor for y in x]
-
-    def plus(x, y, factor):
-        return [u + v * factor for u, v in zip(x, y)]
-
     put_rows(sg_hi, sg_lo, 7, joined(r1, pair_rows(g_ext, 2)))
     put_rows(sg_hi, sg_lo, 8, joined(pair_rows(g_ext, 9), r10))
     put_rows(sg_hi, sg_lo, 9, joined(plus(pair_rows(g_ext, 2), r0, northf), plus(pair_rows(g_ext, 3), r1, northf)))
@@ -471,28 +532,14 @@
     put_rows(sg_hi, sg_lo, 12, joined(plus(pair_rows(g_ext, 8), r10, southf), plus(pair_rows(g_ext, 9), r11, southf)))
     put2((((9, 11),), ((7, 9),), ((11, 13),)), ((0, 0, 2), (2, 8, 2)))
 
-    for m, piece in enumerate(near(p_ext)):
-        q0, q9 = piece[0:1], piece[9:10]
-        for at, part in (
-            (0, piece), (10, piece[2:3] + northf * q0), (11, q9 * (1.0 - southf)),
-            (12, q0 * (1.0 - northf)), (13, piece[7:8] + southf * q9),
-        ):
-            sp_hi[m, at:at + part.shape[0]], sp_lo[m, at:at + part.shape[0]] = halves(part)
-
-    chosen = (((10, 11), (3, 9), (11, 12)), ((1, 9),), ((12, 13), (1, 7), (13, 14)))
-    parts = []
-    for m in range(4):
-        wh, wl, dot = backward(w1_hi, w1_lo, k1)(m)
-        both = dot(taps(sp_hi, chosen)(m), jnp.concatenate([wh, wl], axis=0))
-        parts.append(both[:, :k1] + both[:, k1:] + dot(taps(sp_lo, chosen)(m), wh))
-    m0, m1, m2, m3 = parts
-    for parity, part in enumerate((m0 + m1 + m2, m1 - m2 - m3)):
-        out_v[:, pl.ds(parity, 32, stride=2), :] = part.reshape(8, 32, k1)
-    done = pltpu.make_async_copy(out_v, out, load_sem.at[0])
-    done.start()
+    for m, (q0, q1, q2, q7, q8, q9) in enumerate(zip(*[near_pairs(at, at + 1) for at in (0, 1, 2, 7, 8, 9)])):
+        for at, piece in ((1, q1), (8, q8), (10, q2 + northf * q0), (11, q9 * (1.0 - southf)),
+                          (12, q0 * (1.0 - northf)), (13, q7 + southf * q9)):
+            sp_hi[m, at:at + 1], sp_lo[m, at:at + 1] = halves(piece)
+    put3((((10, 11), (3, 4), (8, 9), (11, 12)), ((1, 3), (7, 9)), ((12, 13), (1, 2), (6, 7), (13, 14))),
+         ((0, 2), (6, 8)))
     for copy in rim2:
         copy.wait_send()
-    done.wait()
 
 
 def shards(n_lon, n_lat, latent, conv1_weight, conv1_bias, conv2_weight, conv2_bias, head_weight, head_bias, land_sea,
@@ -518,31 +565,33 @@
         vmem((1, variables), F32),
         vmem((1, padded), jnp.int32), vmem((1, padded), jnp.int32), vmem((1, padded), jnp.int32),
         vmem((slots, patch), F32), vmem((slots, patch), BF16), vmem((slots, patch), BF16),
+        vmem((2 * slots, patch), BF16),
         vmem((128, patch), BF16), vmem((1, patch), F32),
         vmem((n_lat * CAP, 512), BF16), vmem((512, n_lat * CAP), BF16), vmem((512, rows), BF16),
         vmem((rows, 128), BF16),
+        vmem((128, n_lat * LCAP), BF16), vmem((128, 128), F32),
         vmem((n_lat, LCAP, 128), F32), vmem((n_lat, LCAP, 128), F32),
         vmem((n_lat, MSG, 128), F32), vmem((n_lat, MSG, 128), F32),
         vmem((hid // 128, 12, BUF, 128), F32),
         vmem((4, 13, 2 * PAIRS, hid), BF16), vmem((4, 13, 2 * PAIRS, hid), BF16),
         vmem((2, 10, PAIRS, hid), F32),
         vmem((4, 14, 32, hid), BF16), vmem((4, 14, 32, hid), BF16),
-        vmem((8, 64, lc), F32),
         pltpu.SemaphoreType.DMA((14,)),
-        pltpu.SemaphoreType.DMA((8,)), pltpu.SemaphoreType.DMA((9,)),
-        pltpu.SemaphoreType.DMA((8,)), pltpu.SemaphoreType.DMA((9,)),
+        pltpu.SemaphoreType.DMA((10,)), pltpu.SemaphoreType.DMA((18,)),
+        pltpu.SemaphoreType.DMA((10,)), pltpu.SemaphoreType.DMA((18,)),
     ] + [pltpu.SemaphoreType.DMA((n_lat,))] * 4
     return pl.pallas_call(
         functools.partial(kernel, n_lon, n_lat, slots, patch, variables),
         out_shape=jax.ShapeDtypeStruct(latent.shape, F32),
         in_specs=[pl.BlockSpec(memory_space=pl.ANY)] * 14,
-        out_specs=pl.BlockSpec(memory_space=pl.ANY),
+        out_specs=pl.BlockSpec(memory_space=pltpu.VMEM),
         scratch_shapes=scratch,
         compiler_params=pltpu.CompilerParams(
-            collective_id=0, has_side_effects=True, vmem_limit_bytes=60 * 1024 * 1024),
-    )(latent, conv1_weight.reshape(9 * lc, hid), conv1_bias.reshape(1, hid), conv2_weight.reshape(9 * hid, hid),
+            collective_id=0, has_side_effects=True, vmem_limit_bytes=48 * 1024 * 1024),
+    )(*(pltpu.with_memory_space_constraint(x, pltpu.HBM) for x in (
+        latent, conv1_weight.reshape(9 * lc, hid), conv1_bias.reshape(1, hid), conv2_weight.reshape(9 * hid, hid),
       conv2_bias.reshape(1, hid), head_weight.T, head_bias, land_sea, var_ok,
-      obs_error.reshape(1, variables), obs_band.reshape(1, listed), obs_cell, obs_count, obs_value[0])
+      obs_error.reshape(1, variables), obs_band.reshape(1, listed), obs_cell, obs_count, obs_value[0])))
 
 
 def solution(mesh):

time: 42.2 us -> 40.1 us (0.950)
  the two profiles are of different devices: /device:TPU:1 before, /device:TPU:24 now
where the time goes in v3:
time: 40.1 us; the launch traced here: 40 us
  Pallas kernels  39.3 us (98%)
  local copies, waits for them, and re-layouts  0.71 us (2%)
    pallas_call x1, Pallas kernels, shards(): pl.pallas_call(functools.partial(kernel, n_lon, n_lat, slots, patch, vari...  39.3 us

profile of v3, /device:TPU:24, one launch (start us, length us, event | category | flops | bytes accessed | tf_op | source)
XLA Modules:
  0.0 40.0 jit_solution(1595344175571386428)
XLA Ops:
  0.0 39.3 %shard_map.136 = f32[8,64,128]{2,1,0:T(8,128)S(1)} custom-call(f32[8,64,128]{2,1,0:T(8,128)} %latent.1, f32[1152,256]{1,0:T(8,128)} %bitcast.11, f32[1,256]{1,0:T(1,128)} %bitcast.13, f32[2304,256]{1,0:T(8,128)} %bitcast.9, f32[1,256]{1,0:T(1,128)} %bitcast.14, f32[4416,256]{1,0:T(8,128)} %bitcast.8, f32[4416]{0:T(1024)} %hbias.1, s32[64,512]{1,0:T(8,128)} %land.1, ...), custom_call_target="tpu_custom_call" | custom-call | tf_op jit(solution)/shard_map/pallas_call | solution.py:583
  39.3 0.7 %copy.16 = f32[8,64,128]{2,1,0:T(8,128)} copy(f32[8,64,128]{2,1,0:T(8,128)S(1)} %shard_map.136) | data formatting | bytes 524288

commit v4 on v3

--- a/solution.py
+++ b/solution.py
@@ -52,7 +52,7 @@
     pre1, act1, sb_hi, sb_lo, pre2, head_v, head_hi, head_lo, hb_v, land_v, ok_v, err_v,
     band_v, cell_v, count_v, value_v, val_hi, val_lo, masked, ok_rows, inv_row,
     oh, oht, oht_msg, pmt, from_land, own_weight, land_send, land_recv, term_send, term_recv,
-    g_ext, sg_hi, sg_lo, p_ext, sp_hi, sp_lo,
+    g_ext, side_send, side_recv, corner_send, corner_recv, sg_hi, sg_lo, p_ext, sp_hi, sp_lo,
     load_sem, h_send, h_recv, g_send, g_recv, l_send, l_recv, t_send, t_recv,
 ):
     lon, lat = lax.axis_index("lon"), lax.axis_index("lat")
@@ -148,9 +148,9 @@
                 sent.append(copy)
         return sent
 
-    def rim_arrived(buf, recv_sem, send_sem, kinds):
+    def rim_arrived(buf, recv_sem, send_sem, kinds, drs=(-1, 0, 1)):
         for number, (kind, dr, dc, device) in enumerate(parts):
-            if kind not in kinds:
+            if kind not in kinds or dr not in drs:
                 continue
             cols_ = (0, SIDE) if dc < 0 else (72, SIDE) if dc > 0 else (SIDE, 64)
             second = 1 if kind == far_rows else 0
@@ -168,6 +168,56 @@
                 src_ref=ref, dst_ref=ref, send_sem=send_sem.at[number], recv_sem=recv_sem.at[slot],
                 device_id=device, device_id_type=MESH).wait_recv()
 
+    def last_columns(dc):
+        return SIDE if dc < 0 else SIDE + 62
+
+    def halo_columns(dc):
+        return SIDE - 2 if dc < 0 else 72
+
+    def packed_rim(kind, send_sem, recv_sem):
+        sent = []
+        for number, (its, dr, dc, device) in enumerate(parts):
+            if its != kind:
+                continue
+            at = last_columns(dc)
+            if kind == sides:
+                mine_, theirs_, ref, into_ref = (dc + 1) // 2, (1 - dc) // 2, side_send, side_recv
+                for h in range(hid // 128):
+                    for j in range(2):
+                        ref[mine_, h, 8 * j:8 * j + 8, :] = g_ext[h, 2:10, at + j:at + j + 1, :].reshape(8, 128)
+                slot = 3 + (1 - dc)
+            else:
+                side = 2 - 2 * north if dr < 0 else 2 * south
+                mine_, theirs_, ref, into_ref = dr + 1 + (dc + 1) // 2, side + (1 - dc) // 2, corner_send, corner_recv
+                for h in range(hid // 128):
+                    for r in range(2):
+                        row_ = (2 if dr < 0 else 8) + r
+                        ref[mine_, h, 2 * r:2 * r + 2, :] = g_ext[h, row_, at:at + 2, :]
+                slot = side * 3 + (1 - dc)
+            copy = pltpu.make_async_remote_copy(
+                src_ref=ref.at[mine_], dst_ref=into_ref.at[theirs_], send_sem=send_sem.at[number],
+                recv_sem=recv_sem.at[slot], device_id=device, device_id_type=MESH)
+            copy.start()
+            sent.append(copy)
+        return sent
+
+    def packed_arrived(kind, its_dr, send_sem, recv_sem):
+        for number, (its, dr, dc, device) in enumerate(parts):
+            if its != kind or dr != its_dr:
+                continue
+            at, slot = halo_columns(dc), (dr + 1) * 3 + dc + 1
+            mine_ = (dc + 1) // 2 if kind == sides else dr + 1 + (dc + 1) // 2
+            ref = side_recv if kind == sides else corner_recv
+            pltpu.make_async_remote_copy(
+                src_ref=ref.at[mine_], dst_ref=ref.at[mine_], send_sem=send_sem.at[number],
+                recv_sem=recv_sem.at[slot], device_id=device, device_id_type=MESH).wait_recv()
+            for h in range(hid // 128):
+                for j in range(2):
+                    if kind == sides:
+                        g_ext[h, 2:10, at + j:at + j + 1, :] = ref[mine_, h, 8 * j:8 * j + 8, :].reshape(8, 1, 128)
+                    else:
+                        g_ext[h, (0 if dr < 0 else 10) + j, at:at + 2, :] = ref[mine_, h, 2 * j:2 * j + 2, :]
+
     def exchange(src, dst, send_sem, recv_sem):
         sent = []
         for number, peer in enumerate(peers):
@@ -226,11 +276,15 @@
         put_rows(high_ref, low_ref, 0, pieces)
         put_rows(high_ref, low_ref, 4, [x[1:7] for x in pieces])
 
-    def pair_sums(taken_hi, taken_lo, weights):
+    def pair_sums(taken_hi, taken_lo, weights, stacked=False):
         products = []
         for m in range(4):
             lhs, (wh, wl, dot) = taken_hi(m), weights(m)
-            products.append(dot(lhs, wh) + dot(lhs, wl) + dot(taken_lo(m), wh))
+            if stacked:
+                both_ = dot(jnp.concatenate([lhs, taken_lo(m)], axis=0), wh)
+                products.append(both_[:lhs.shape[0]] + both_[lhs.shape[0]:] + dot(lhs, wl))
+            else:
+                products.append(dot(lhs, wh) + dot(lhs, wl) + dot(taken_lo(m), wh))
         m0, m1, m2, m3 = products
         return m0 + m1 + m2, m1 - m2 - m3
 
@@ -241,7 +295,7 @@
         return lhs
 
     lat_ext[:, :, 80:88, :] = jnp.zeros((k1 // 128, 12, 8, 128), F32)
-    g_ext[:, :, 80:88, :] = jnp.zeros((hid // 128, 12, 8, 128), F32)
+    g_ext[:, :, 72:88, :] = jnp.zeros((hid // 128, 12, 16, 128), F32)
 
     ld_band.wait()
     ld_cell.wait()
@@ -367,14 +421,6 @@
 
     inner_rows(lat_ext, sa_hi, sa_lo)
     put1((((0, 3),), ((4, 7),), ((1, 4),)), ((0, 2, 6),))
-    rim_arrived(lat_ext, h_recv, h_send, (near_rows, corners, far_rows))
-    for at, one, other in (
-        (7, 1 - north, 2), (8, 9, 10 + south),
-        (9, 2 * north, 1 - north), (10, 8, 9 + south),
-        (11, 2 - north, 3), (12, 10 + south, 11 - 2 * south),
-    ):
-        put_rows(sa_hi, sa_lo, at, joined(pair_rows(lat_ext, one), pair_rows(lat_ext, other)))
-    put1((((9, 11),), ((7, 9),), ((11, 13),)), ((0, 0, 2), (2, 8, 2)))
 
     arrived(land_recv, l_send, l_recv)
     flags_own = nn(from_land[...], land_recv[...].reshape(lrows, 128).astype(BF16))
@@ -408,6 +454,15 @@
     term_send[...] = jnp.where(upper, sent_terms[:, :128], sent_terms[:, 128:]).reshape(n_lat, MSG, 128)
     terms_sent = exchange(term_send, term_recv, t_send, t_recv)
 
+    rim_arrived(lat_ext, h_recv, h_send, (near_rows, corners, far_rows))
+    for at, one, other in (
+        (7, 1 - north, 2), (8, 9, 10 + south),
+        (9, 2 * north, 1 - north), (10, 8, 9 + south),
+        (11, 2 - north, 3), (12, 10 + south, 11 - 2 * south),
+    ):
+        put_rows(sa_hi, sa_lo, at, joined(pair_rows(lat_ext, one), pair_rows(lat_ext, other)))
+    put1((((9, 11),), ((7, 9),), ((11, 13),)), ((0, 0, 2), (2, 8, 2)))
+
     def near(ref, rows_=slice(0, 10)):
         return factors(ref[0, rows_, 0:32], ref[1, rows_, 0:32], ref[0, rows_, 1:33], ref[1, rows_, 1:33])
 
@@ -467,13 +522,14 @@
                         grad2[:, 128 * h:128 * h + 128].reshape(last - first_, 32, 128))
 
     put_grad(((0, 2), (6, 8)))
-    rim2 = rim(g_ext, g_send, g_recv, (near_rows, corners, far_rows))
+    rim2 = rim(g_ext, g_send, g_recv, (near_rows, far_rows))
+    rim2 += packed_rim(corners, g_send, g_recv)
     put_grad(((2, 6),))
-    rim2 += rim(g_ext, g_send, g_recv, (sides,))
+    rim2 += packed_rim(sides, g_send, g_recv)
     for copy in terms_sent:
         copy.wait_send()
 
-    rim_arrived(g_ext, g_recv, g_send, (sides,))
+    packed_arrived(sides, 0, g_send, g_recv)
 
     def backward(high_ref, low_ref, depth):
         def weights(m):
@@ -482,8 +538,8 @@
                          for ref in (high_ref, low_ref)) + (nt,)
         return weights
 
-    def put2(chosen, groups):
-        sums = pair_sums(taps(sg_hi, chosen), taps(sg_lo, chosen), backward(w2_hi, w2_lo, hid))
+    def put2(chosen, groups, stacked=False):
+        sums = pair_sums(taps(sg_hi, chosen), taps(sg_lo, chosen), backward(w2_hi, w2_lo, hid), stacked)
         for parity, grad1 in enumerate(sums):
             for source, target, length in groups:
                 part = grad1[source * PAIRS:(source + length) * PAIRS].reshape(length, PAIRS, hid)
@@ -507,8 +563,10 @@
         products = []
         for m in range(4):
             wh, wl, dot = backward(w1_hi, w1_lo, k1)(m)
-            both_ = dot(taps(sp_hi, chosen)(m), jnp.concatenate([wh, wl], axis=0))
-            products.append(both_[:, :k1] + both_[:, k1:] + dot(taps(sp_lo, chosen)(m), wh))
+            lhs = taps(sp_hi, chosen)(m)
+            count_ = lhs.shape[0]
+            both_ = dot(jnp.concatenate([lhs, taps(sp_lo, chosen)(m)], axis=0), jnp.concatenate([wh, wl], axis=0))
+            products.append(both_[:count_, :k1] + both_[:count_, k1:] + both_[count_:, :k1])
         m0, m1, m2, m3 = products
         for parity, part in enumerate((m0 + m1 + m2, m1 - m2 - m3)):
             part = part.reshape(part.shape[0] // 32, 32, k1)
@@ -521,23 +579,29 @@
     put2((((1, 4),), ((4, 7),), ((0, 3),)), ((0, 2, 6),))
     put_pairs(2, 8, 2)
     put3((((4, 8),), ((3, 7),), ((2, 6),)), ((2, 6),))
-    rim_arrived(g_ext, g_recv, g_send, (near_rows, corners, far_rows))
+    rim_arrived(g_ext, g_recv, g_send, (near_rows, far_rows), (1,))
+    packed_arrived(corners, 1, g_send, g_recv)
+    r10, r11 = pair_rows(g_ext, 10 + south), pair_rows(g_ext, 11 - south)
+    put_rows(sg_hi, sg_lo, 8, joined(pair_rows(g_ext, 9), r10))
+    put_rows(sg_hi, sg_lo, 10, joined(scaled_by(r10, 1.0 - southf), scaled_by(r11, 1.0 - southf)))
+    put_rows(sg_hi, sg_lo, 12, joined(plus(pair_rows(g_ext, 8), r10, southf), plus(pair_rows(g_ext, 9), r11, southf)))
+    put2((((10, 11),), ((8, 9),), ((12, 13),)), ((0, 8, 2),), True)
+    for m, (q7, q8, q9) in enumerate(zip(*[near_pairs(at, at + 1) for at in (7, 8, 9)])):
+        for at, piece in ((8, q8), (11, q9 * (1.0 - southf)), (13, q7 + southf * q9)):
+            sp_hi[m, at:at + 1], sp_lo[m, at:at + 1] = halves(piece)
+    put3((((8, 9), (11, 12)), ((7, 9),), ((6, 7), (13, 14))), ((6, 8),))
+
+    rim_arrived(g_ext, g_recv, g_send, (near_rows, far_rows), (-1,))
+    packed_arrived(corners, -1, g_send, g_recv)
     r0, r1 = pair_rows(g_ext, north), pair_rows(g_ext, 1 - north)
-    r10, r11 = pair_rows(g_ext, 10 + south), pair_rows(g_ext, 11 - south)
     put_rows(sg_hi, sg_lo, 7, joined(r1, pair_rows(g_ext, 2)))
-    put_rows(sg_hi, sg_lo, 8, joined(pair_rows(g_ext, 9), r10))
     put_rows(sg_hi, sg_lo, 9, joined(plus(pair_rows(g_ext, 2), r0, northf), plus(pair_rows(g_ext, 3), r1, northf)))
-    put_rows(sg_hi, sg_lo, 10, joined(scaled_by(r10, 1.0 - southf), scaled_by(r11, 1.0 - southf)))
     put_rows(sg_hi, sg_lo, 11, joined(scaled_by(r0, 1.0 - northf), scaled_by(r1, 1.0 - northf)))
-    put_rows(sg_hi, sg_lo, 12, joined(plus(pair_rows(g_ext, 8), r10, southf), plus(pair_rows(g_ext, 9), r11, southf)))
-    put2((((9, 11),), ((7, 9),), ((11, 13),)), ((0, 0, 2), (2, 8, 2)))
-
-    for m, (q0, q1, q2, q7, q8, q9) in enumerate(zip(*[near_pairs(at, at + 1) for at in (0, 1, 2, 7, 8, 9)])):
-        for at, piece in ((1, q1), (8, q8), (10, q2 + northf * q0), (11, q9 * (1.0 - southf)),
-                          (12, q0 * (1.0 - northf)), (13, q7 + southf * q9)):
+    put2((((9, 10),), ((7, 8),), ((11, 12),)), ((0, 0, 2),), True)
+    for m, (q0, q1, q2) in enumerate(zip(*[near_pairs(at, at + 1) for at in (0, 1, 2)])):
+        for at, piece in ((1, q1), (10, q2 + northf * q0), (12, q0 * (1.0 - northf))):
             sp_hi[m, at:at + 1], sp_lo[m, at:at + 1] = halves(piece)
-    put3((((10, 11), (3, 4), (8, 9), (11, 12)), ((1, 3), (7, 9)), ((12, 13), (1, 2), (6, 7), (13, 14))),
-         ((0, 2), (6, 8)))
+    put3((((10, 11), (3, 4)), ((1, 3),), ((12, 13), (1, 2))), ((0, 2),))
     for copy in rim2:
         copy.wait_send()
 
@@ -573,6 +637,8 @@
         vmem((n_lat, LCAP, 128), F32), vmem((n_lat, LCAP, 128), F32),
         vmem((n_lat, MSG, 128), F32), vmem((n_lat, MSG, 128), F32),
         vmem((hid // 128, 12, BUF, 128), F32),
+        vmem((2, hid // 128, 16, 128), F32), vmem((2, hid // 128, 16, 128), F32),
+        vmem((4, hid // 128, 4, 128), F32), vmem((4, hid // 128, 4, 128), F32),
         vmem((4, 13, 2 * PAIRS, hid), BF16), vmem((4, 13, 2 * PAIRS, hid), BF16),
         vmem((2, 10, PAIRS, hid), F32),
         vmem((4, 14, 32, hid), BF16), vmem((4, 14, 32, hid), BF16),

time: 40.1 us -> 39 us (0.973)
  the two profiles are of different devices: /device:TPU:24 before, /device:TPU:1 now
where the time goes in v4:
time: 39 us; the launch traced here: 38.8 us
  Pallas kernels  38.1 us (98%)
  local copies, waits for them, and re-layouts  0.71 us (2%)
    pallas_call x1, Pallas kernels, shards(): pl.pallas_call(functools.partial(kernel, n_lon, n_lat, slots, patch, vari...  38.1 us

profile of v4, /device:TPU:1, one launch (start us, length us, event | category | flops | bytes accessed | tf_op | source)
XLA Modules:
  0.0 38.8 jit_solution(4369047981583212781)
XLA Ops:
  0.0 38.1 %shard_map.136 = f32[8,64,128]{2,1,0:T(8,128)S(1)} custom-call(f32[8,64,128]{2,1,0:T(8,128)} %latent.1, f32[1152,256]{1,0:T(8,128)} %bitcast.11, f32[1,256]{1,0:T(1,128)} %bitcast.13, f32[2304,256]{1,0:T(8,128)} %bitcast.9, f32[1,256]{1,0:T(1,128)} %bitcast.14, f32[4416,256]{1,0:T(8,128)} %bitcast.8, f32[4416]{0:T(1024)} %hbias.1, s32[64,512]{1,0:T(8,128)} %land.1, ...), custom_call_target="tpu_custom_call" | custom-call | tf_op jit(solution)/shard_map/pallas_call | solution.py:649
  38.1 0.7 %copy.16 = f32[8,64,128]{2,1,0:T(8,128)} copy(f32[8,64,128]{2,1,0:T(8,128)S(1)} %shard_map.136) | data formatting | bytes 524288

commit v5 on v4

--- a/solution.py
+++ b/solution.py
@@ -12,6 +12,7 @@
 CAP = 12
 MSG = 2 * CAP
 LCAP = 16
+GROUPS = ((0, 2, 0), (6, 8, 128), (2, 6, 256))
 SIDE = 8
 PAIRS = 40
 BUF = 88
@@ -51,7 +52,7 @@
     lat_ext, sa_hi, sa_lo, w1_v, w1_hi, w1_lo, w2_v, w2_hi, w2_lo, b1_v, b2_v,
     pre1, act1, sb_hi, sb_lo, pre2, head_v, head_hi, head_lo, hb_v, land_v, ok_v, err_v,
     band_v, cell_v, count_v, value_v, val_hi, val_lo, masked, ok_rows, inv_row,
-    oh, oht, oht_msg, pmt, from_land, own_weight, land_send, land_recv, term_send, term_recv,
+    tiles_v, flags_w, oh, oht, oht_msg, pmt, from_land, own_weight, land_send, land_recv, term_send, term_recv,
     g_ext, side_send, side_recv, corner_send, corner_recv, sg_hi, sg_lo, p_ext, sp_hi, sp_lo,
     load_sem, h_send, h_recv, g_send, g_recv, l_send, l_recv, t_send, t_recv,
 ):
@@ -118,17 +119,17 @@
         else:
             parts.append((corners if dr else sides, dr, dc, device))
 
-    def rim(buf, send_sem, recv_sem, kinds):
+    def rim(buf, send_sem, recv_sem, kinds, drs=(-1, 0, 1)):
         sent = []
         for kind in kinds:
             for number, (its, dr, dc, device) in enumerate(parts):
-                if its != kind:
+                if its != kind or dr not in drs:
                     continue
                 src_c = (SIDE, SIDE) if dc < 0 else (SIDE + 56, SIDE) if dc > 0 else (SIDE, 64)
                 dst_c = 72 if dc < 0 else 0 if dc > 0 else SIDE
                 second = 1 if kind == far_rows else 0
                 if dr < 0:
-                    src_r, dst_r, side = 2 + second, 10 - 10 * north + second, 2 - 2 * north
+                    src_r, dst_r, side = 2 + second, 10 - 10 * north + second, 2 * (1 - north)
                 elif dr > 0:
                     src_r, dst_r, side = 9 - second, 1 + 10 * south - second, 2 * south
                 else:
@@ -138,7 +139,7 @@
                     length = 2
                     if dr > 0:
                         src_r, dst_r = 8, 10 * south
-                slot = 9 * second + side * 3 + (1 - dc)
+                slot = 9 + (1 - north if dr < 0 else south) if second else side * 3 + (1 - dc)
                 src = buf.at[:, pl.ds(src_r, length), pl.ds(src_c[0], src_c[1]), :]
                 dst = buf.at[:, pl.ds(dst_r, length), pl.ds(dst_c, src_c[1]), :]
                 copy = pltpu.make_async_remote_copy(
@@ -163,7 +164,7 @@
                 if second:
                     at = north if dr < 0 else 11 - south
             ref = buf.at[:, pl.ds(at, length), pl.ds(cols_[0], cols_[1]), :]
-            slot = 9 * second + (dr + 1) * 3 + dc + 1
+            slot = 9 + (dr + 1) // 2 if second else (dr + 1) * 3 + dc + 1
             pltpu.make_async_remote_copy(
                 src_ref=ref, dst_ref=ref, send_sem=send_sem.at[number], recv_sem=recv_sem.at[slot],
                 device_id=device, device_id_type=MESH).wait_recv()
@@ -174,10 +175,10 @@
     def halo_columns(dc):
         return SIDE - 2 if dc < 0 else 72
 
-    def packed_rim(kind, send_sem, recv_sem):
+    def packed_rim(kind, its_dr, send_sem, recv_sem):
         sent = []
         for number, (its, dr, dc, device) in enumerate(parts):
-            if its != kind:
+            if its != kind or dr != its_dr:
                 continue
             at = last_columns(dc)
             if kind == sides:
@@ -219,21 +220,15 @@
                         g_ext[h, (0 if dr < 0 else 10) + j, at:at + 2, :] = ref[mine_, h, 2 * j:2 * j + 2, :]
 
     def exchange(src, dst, send_sem, recv_sem):
-        sent = []
-        for number, peer in enumerate(peers):
-            copy = pltpu.make_async_remote_copy(
-                src_ref=src.at[peer], dst_ref=dst.at[lat], send_sem=send_sem.at[number], recv_sem=recv_sem.at[lat],
-                device_id=(lon, peer), device_id_type=MESH)
-            copy.start()
-            sent.append(copy)
+        for peer in peers:
+            pltpu.make_async_remote_copy(
+                src_ref=src.at[peer], dst_ref=dst.at[lat], send_sem=send_sem.at[0], recv_sem=recv_sem.at[0],
+                device_id=(lon, peer), device_id_type=MESH).start()
         dst[pl.ds(lat, 1)] = src[pl.ds(lat, 1)]
-        return sent
-
-    def arrived(dst, send_sem, recv_sem):
-        for number, peer in enumerate(peers):
-            pltpu.make_async_remote_copy(
-                src_ref=dst.at[peer], dst_ref=dst.at[peer], send_sem=send_sem.at[number], recv_sem=recv_sem.at[peer],
-                device_id=(lon, peer), device_id_type=MESH).wait_recv()
+        every = pl.ds(0, len(peers))
+        return pltpu.make_async_remote_copy(
+            src_ref=src.at[every], dst_ref=dst.at[every], send_sem=send_sem.at[0], recv_sem=recv_sem.at[0],
+            device_id=(lon, peers[0]), device_id_type=MESH)
 
     def split(src, high_ref, low_ref, step):
         def body(i, carry):
@@ -312,10 +307,45 @@
     below = below.astype(F32).astype(BF16)
     mine = jnp.where(live & (bands == lat), 1.0, 0.0)
     pick = jnp.where(mine > 0.0, nn(mine.astype(BF16), below), -1.0)
-    cells = ((cells >> 6) << 5) + ((cells & 63) >> 1) + ((cells & 1) << 8)
+    cell_row, odd, pair = cells >> 6, cells & 1, (cells & 63) >> 1
+    edge = (cell_row << 5) + (odd << 6) + jnp.where(cell_row > 5, 128 - 6 * 32, 0)
+    inner = (cell_row << 5) + (odd << 7) + (256 - 2 * 32)
+    cells = pair + jnp.where((cell_row < 2) | (cell_row > 5), edge, inner)
     cellsf = cells.astype(F32) + 1.0
     countsf = counts.astype(F32) * 0.125
     msg_k = lax.rem(lax.broadcasted_iota(jnp.int32, (MSG, 128), 0), CAP).astype(F32)
+    land_k = lax.broadcasted_iota(jnp.int32, (LCAP, 128), 0).astype(F32)
+    named = [jnp.sum(jnp.where(pick[a:a + 1] == land_k, cellsf[a:a + 1], 0.0), axis=1, keepdims=True)
+             for a in range(n_lat)]
+    wanted = jnp.concatenate(named, axis=0).astype(jnp.int32) - 1
+    lrows = n_lat * LCAP
+    messages = jnp.where(wanted == lax.broadcasted_iota(jnp.int32, (lrows, 512), 1), 1.0, 0.0).astype(BF16)
+
+    ld_land.wait()
+    column = lax.broadcasted_iota(jnp.int32, (64, 512), 0)
+    column = ((column & 31) << 1) + (column >> 5)
+    fold = (lax.broadcasted_iota(jnp.int32, (64, 512), 1) >> 3) == column
+    fold = jnp.where(fold, 1.0, 0.0).astype(BF16)
+    kept = (lax.broadcasted_iota(jnp.int32, (8, 512), 1) & 7) == lax.broadcasted_iota(jnp.int32, (8, 512), 0)
+    tiles = []
+    for r in range(8):
+        strip = land_v[8 * r:8 * r + 8, :].astype(F32)
+        spread = jnp.concatenate([jnp.where(kept, strip[p:p + 1], 0.0) for p in range(8)], axis=0)
+        tiles.append(nt(fold, spread.astype(BF16)))
+    tiles = [tiles[r][32 * parity:32 * parity + 32] for first_, last, _ in GROUPS for parity in range(2) for r in range(first_, last)]
+    tiles = jnp.concatenate(tiles, axis=0)
+    tiles = jnp.concatenate([tiles, 1.0 - tiles], axis=1).astype(BF16)
+    tiles_v[...] = tiles
+    land_send[...] = nn(messages, tiles).reshape(n_lat, LCAP, 128)
+
+    pl.semaphore_wait(barrier, len(around) + len(peers))
+    land_sent = exchange(land_send, land_recv, l_send, l_recv)
+    ld_lat.wait()
+    rim1 = rim(lat_ext, h_send, h_recv, (sides, near_rows, corners, far_rows))
+
+    ld_w1.wait()
+    split_taps(w1_v, w1_hi, w1_lo, k1, 64)
+
     first = lax.broadcasted_iota(jnp.int32, (MSG, 128), 0) < CAP
     taken = n_lat * CAP
     named, merged = [], []
@@ -328,42 +358,13 @@
     wanted = jnp.concatenate(named, axis=0).astype(jnp.int32) - 1
     weight = jnp.concatenate(merged, axis=0)
     oh[...] = jnp.where(wanted == lax.broadcasted_iota(jnp.int32, (taken, 512), 1), 1.0, 0.0).astype(BF16)
-
-    ld_land.wait()
-    column = lax.broadcasted_iota(jnp.int32, (64, 512), 0)
-    column = ((column & 31) << 1) + (column >> 5)
-    fold = (lax.broadcasted_iota(jnp.int32, (64, 512), 1) >> 3) == column
-    fold = jnp.where(fold, 1.0, 0.0).astype(BF16)
-    kept = (lax.broadcasted_iota(jnp.int32, (8, 512), 1) & 7) == lax.broadcasted_iota(jnp.int32, (8, 512), 0)
-    tiles = []
-    for r in range(8):
-        strip = land_v[8 * r:8 * r + 8, :].astype(F32)
-        spread = jnp.concatenate([jnp.where(kept, strip[p:p + 1], 0.0) for p in range(8)], axis=0)
-        tiles.append(nt(fold, spread.astype(BF16)))
-    tiles = jnp.concatenate([x[:32] for x in tiles] + [x[32:] for x in tiles], axis=0)
-    tiles = jnp.concatenate([tiles, 1.0 - tiles], axis=1).astype(BF16)
-    flags = nn(oh[...], tiles)
-    lrows = n_lat * LCAP
-    row = lax.broadcasted_iota(jnp.int32, (lrows, taken), 0)
-    into = (row & (LCAP - 1)) + (row >> 4) * CAP == lax.broadcasted_iota(jnp.int32, (lrows, taken), 1)
-    into = into & ((row & (LCAP - 1)) < CAP)
-    land_send[...] = nn(jnp.where(into, 1.0, 0.0).astype(BF16), flags.astype(BF16)).reshape(n_lat, LCAP, 128)
-    flags_w = (flags * weight).astype(BF16)
-
-    pl.semaphore_wait(barrier, len(around) + len(peers))
-    land_sent = exchange(land_send, land_recv, l_send, l_recv)
-    ld_lat.wait()
-    rim1 = rim(lat_ext, h_send, h_recv, (sides, near_rows, corners, far_rows))
-
-    ld_w1.wait()
-    split_taps(w1_v, w1_hi, w1_lo, k1, 64)
+    flags_w[...] = (nn(oh[...], tiles_v[...]) * weight).astype(BF16)
 
     own = lax.broadcasted_iota(jnp.int32, (n_lat, 128), 0) == lat
     own_band = jnp.sum(jnp.where(own, bands, 0), axis=0, keepdims=True)
     own_count = jnp.sum(jnp.where(own, countsf, 0.0), axis=0, keepdims=True)
     theirs = jnp.where(live & (own_band == lax.broadcasted_iota(jnp.int32, (n_lat, 128), 0)), 1.0, 0.0)
     place = jnp.where(theirs > 0.0, nn(theirs.astype(BF16), below), -1.0)
-    land_k = lax.broadcasted_iota(jnp.int32, (LCAP, 128), 0).astype(F32)
     pmt[...] = jnp.concatenate(
         [jnp.where(place[b:b + 1] == msg_k, 1.0, 0.0) for b in range(n_lat)], axis=0).astype(BF16)
     pml = jnp.concatenate([jnp.where(place[b:b + 1] == land_k, 1.0, 0.0) for b in range(n_lat)], axis=0)
@@ -422,7 +423,7 @@
     inner_rows(lat_ext, sa_hi, sa_lo)
     put1((((0, 3),), ((4, 7),), ((1, 4),)), ((0, 2, 6),))
 
-    arrived(land_recv, l_send, l_recv)
+    land_sent.wait_recv()
     flags_own = nn(from_land[...], land_recv[...].reshape(lrows, 128).astype(BF16))
     flags_own = flags_own[:slots].astype(BF16)
 
@@ -473,7 +474,9 @@
         return w2_hi[m], w2_lo[m], nn
 
     chosen = tuple(((i, i + 8),) for i in range(3))
-    summed = jnp.concatenate(pair_sums(taps(sb_hi, chosen), taps(sb_lo, chosen), forward2), axis=0) + b2_v[...]
+    summed = pair_sums(taps(sb_hi, chosen), taps(sb_lo, chosen), forward2)
+    summed = [x[32 * first_:32 * last] for first_, last, _ in GROUPS for x in summed]
+    summed = jnp.concatenate(summed, axis=0) + b2_v[...]
     pre2[...] = summed
     act2, _ = gelu_parts(summed)
 
@@ -486,7 +489,7 @@
         span = slice(at, at + size)
         both = nt(cols_both, head_hi[span, :])
         decoded = both[:taken] + both[taken:] + nt(cols_hi, head_lo[span, :])
-        high, low = halves(nn(flags_w, ok_rows[:, span]) * inv_row[:, span] * decoded)
+        high, low = halves(nn(flags_w[...], ok_rows[:, span]) * inv_row[:, span] * decoded)
         terms = back(high, low, at, size, terms)
 
     wanted_row = jnp.transpose(jnp.broadcast_to(wanted.astype(F32), (taken, 128)))[0:1, :].astype(jnp.int32)
@@ -501,33 +504,33 @@
     hidden = hidden[:, :hid] + hidden[:, hid:]
     pre2[...] = gelu_slope(pre2[...])
     pre1[...] = gelu_slope(pre1[...])
-    for copy in rim1 + land_sent:
+    for copy in rim1:
         copy.wait_send()
-
-    arrived(term_recv, t_send, t_recv)
+    land_sent.wait_send()
+
+    terms_sent.wait_recv()
 
     came = term_recv[...].reshape(rows, 128)
     came = jnp.concatenate([jnp.where(upper, came, 0.0), jnp.where(upper, 0.0, came)], axis=1)
     high, low = halves(came)
     came = jnp.concatenate([high, low], axis=1)
 
-    def put_grad(groups):
-        for first_, last in groups:
-            for parity in range(2):
-                cells_ = slice(256 * parity + 32 * first_, 256 * parity + 32 * last)
-                moved = nn(oht_msg[cells_, :], came)
-                grad2 = (hidden[cells_] - moved[:, :hid] - moved[:, hid:]) * pre2[cells_, :]
-                for h in range(hid // 128):
-                    g_ext[h, 2 + first_:2 + last, pl.ds(SIDE + parity, 32, stride=2), :] = (
-                        grad2[:, 128 * h:128 * h + 128].reshape(last - first_, 32, 128))
-
-    put_grad(((0, 2), (6, 8)))
-    rim2 = rim(g_ext, g_send, g_recv, (near_rows, far_rows))
-    rim2 += packed_rim(corners, g_send, g_recv)
-    put_grad(((2, 6),))
-    rim2 += packed_rim(sides, g_send, g_recv)
-    for copy in terms_sent:
-        copy.wait_send()
+    rim2 = []
+    for (first_, last, base), dr in zip(GROUPS, (-1, 1, 0)):
+        held = 32 * (last - first_)
+        cells_ = slice(base, base + 2 * held)
+        moved = nn(oht_msg[cells_, :], came)
+        grad2 = (hidden[cells_] - moved[:, :hid] - moved[:, hid:]) * pre2[cells_, :]
+        for parity in range(2):
+            for h in range(hid // 128):
+                g_ext[h, 2 + first_:2 + last, pl.ds(SIDE + parity, 32, stride=2), :] = (
+                    grad2[held * parity:held * parity + held, 128 * h:128 * h + 128].reshape(last - first_, 32, 128))
+        if dr:
+            rim2 += rim(g_ext, g_send, g_recv, (near_rows, far_rows), (dr,))
+            rim2 += packed_rim(corners, dr, g_send, g_recv)
+        else:
+            rim2 += packed_rim(sides, dr, g_send, g_recv)
+    terms_sent.wait_send()
 
     packed_arrived(sides, 0, g_send, g_recv)
 
@@ -631,6 +634,7 @@
         vmem((slots, patch), F32), vmem((slots, patch), BF16), vmem((slots, patch), BF16),
         vmem((2 * slots, patch), BF16),
         vmem((128, patch), BF16), vmem((1, patch), F32),
+        vmem((512, 128), BF16), vmem((n_lat * CAP, 128), BF16),
         vmem((n_lat * CAP, 512), BF16), vmem((512, n_lat * CAP), BF16), vmem((512, rows), BF16),
         vmem((rows, 128), BF16),
         vmem((128, n_lat * LCAP), BF16), vmem((128, 128), F32),
@@ -643,9 +647,9 @@
         vmem((2, 10, PAIRS, hid), F32),
         vmem((4, 14, 32, hid), BF16), vmem((4, 14, 32, hid), BF16),
         pltpu.SemaphoreType.DMA((14,)),
-        pltpu.SemaphoreType.DMA((10,)), pltpu.SemaphoreType.DMA((18,)),
-        pltpu.SemaphoreType.DMA((10,)), pltpu.SemaphoreType.DMA((18,)),
-    ] + [pltpu.SemaphoreType.DMA((n_lat,))] * 4
+        pltpu.SemaphoreType.DMA((10,)), pltpu.SemaphoreType.DMA((11,)),
+        pltpu.SemaphoreType.DMA((10,)), pltpu.SemaphoreType.DMA((11,)),
+    ] + [pltpu.SemaphoreType.DMA((1,))] * 4
     return pl.pallas_call(
         functools.partial(kernel, n_lon, n_lat, slots, patch, variables),
         out_shape=jax.ShapeDtypeStruct(latent.shape, F32),

time: 39 us -> 38.3 us (0.982)
  Pallas kernels: 38.1 us -> 37.4 us
    pallas_call x1, Pallas kernels: 38.1 us -> 37.4 us  [shards(): pl.pallas_call(functools.partial(kernel, n_lon, n_lat, slots, patch, vari...]
where the time goes in v5:
time: 38.3 us; the launch traced here: 38.2 us
  Pallas kernels  37.4 us (98%)
  local copies, waits for them, and re-layouts  0.71 us (2%)
    pallas_call x1, Pallas kernels, shards(): pl.pallas_call(functools.partial(kernel, n_lon, n_lat, slots, patch, vari...  37.4 us

profile of v5, /device:TPU:1, one launch (start us, length us, event | category | flops | bytes accessed | tf_op | source)
XLA Modules:
  0.0 38.2 jit_solution(15008657871128890025)
XLA Ops:
  0.0 37.4 %shard_map.136 = f32[8,64,128]{2,1,0:T(8,128)S(1)} custom-call(f32[8,64,128]{2,1,0:T(8,128)} %latent.1, f32[1152,256]{1,0:T(8,128)} %bitcast.11, f32[1,256]{1,0:T(1,128)} %bitcast.13, f32[2304,256]{1,0:T(8,128)} %bitcast.9, f32[1,256]{1,0:T(1,128)} %bitcast.14, f32[4416,256]{1,0:T(8,128)} %bitcast.8, f32[4416]{0:T(1024)} %hbias.1, s32[64,512]{1,0:T(8,128)} %land.1, ...), custom_call_target="tpu_custom_call" | custom-call | tf_op jit(solution)/shard_map/pallas_call | solution.py:653
  37.5 0.7 %copy.16 = f32[8,64,128]{2,1,0:T(8,128)} copy(f32[8,64,128]{2,1,0:T(8,128)S(1)} %shard_map.136) | data formatting | bytes 524288

commit v6 on v5

--- a/solution.py
+++ b/solution.py
@@ -111,13 +111,10 @@
     for copy in copies[5:]:
         copy.start()
 
-    near_rows, far_rows, corners, sides = range(4)
+    edges, corners, sides = range(3)
     parts = []
     for dr, dc, device in around:
-        if dr and not dc:
-            parts += [(near_rows, dr, dc, device), (far_rows, dr, dc, device)]
-        else:
-            parts.append((corners if dr else sides, dr, dc, device))
+        parts.append((corners if dr and dc else edges if dr else sides, dr, dc, device))
 
     def rim(buf, send_sem, recv_sem, kinds, drs=(-1, 0, 1)):
         sent = []
@@ -127,19 +124,14 @@
                     continue
                 src_c = (SIDE, SIDE) if dc < 0 else (SIDE + 56, SIDE) if dc > 0 else (SIDE, 64)
                 dst_c = 72 if dc < 0 else 0 if dc > 0 else SIDE
-                second = 1 if kind == far_rows else 0
                 if dr < 0:
-                    src_r, dst_r, side = 2 + second, 10 - 10 * north + second, 2 * (1 - north)
+                    src_r, dst_r, side = 2, 10 - 10 * north, 2 * (1 - north)
                 elif dr > 0:
-                    src_r, dst_r, side = 9 - second, 1 + 10 * south - second, 2 * south
+                    src_r, dst_r, side = 8, 10 * south, 2 * south
                 else:
                     src_r, dst_r, side = 2, 2, 1
-                length = 8 if kind == sides else 1
-                if kind == corners:
-                    length = 2
-                    if dr > 0:
-                        src_r, dst_r = 8, 10 * south
-                slot = 9 + (1 - north if dr < 0 else south) if second else side * 3 + (1 - dc)
+                length = 8 if kind == sides else 2
+                slot = side * 3 + (1 - dc)
                 src = buf.at[:, pl.ds(src_r, length), pl.ds(src_c[0], src_c[1]), :]
                 dst = buf.at[:, pl.ds(dst_r, length), pl.ds(dst_c, src_c[1]), :]
                 copy = pltpu.make_async_remote_copy(
@@ -154,17 +146,9 @@
             if kind not in kinds or dr not in drs:
                 continue
             cols_ = (0, SIDE) if dc < 0 else (72, SIDE) if dc > 0 else (SIDE, 64)
-            second = 1 if kind == far_rows else 0
-            if kind == sides:
-                at, length = 2, 8
-            elif kind == corners:
-                at, length = (0 if dr < 0 else 10), 2
-            else:
-                at, length = (1 - north if dr < 0 else 10 + south), 1
-                if second:
-                    at = north if dr < 0 else 11 - south
+            at, length = (2, 8) if kind == sides else (0 if dr < 0 else 10, 2)
             ref = buf.at[:, pl.ds(at, length), pl.ds(cols_[0], cols_[1]), :]
-            slot = 9 + (dr + 1) // 2 if second else (dr + 1) * 3 + dc + 1
+            slot = (dr + 1) * 3 + dc + 1
             pltpu.make_async_remote_copy(
                 src_ref=ref, dst_ref=ref, send_sem=send_sem.at[number], recv_sem=recv_sem.at[slot],
                 device_id=device, device_id_type=MESH).wait_recv()
@@ -341,7 +325,7 @@
     pl.semaphore_wait(barrier, len(around) + len(peers))
     land_sent = exchange(land_send, land_recv, l_send, l_recv)
     ld_lat.wait()
-    rim1 = rim(lat_ext, h_send, h_recv, (sides, near_rows, corners, far_rows))
+    rim1 = rim(lat_ext, h_send, h_recv, (sides, edges, corners))
 
     ld_w1.wait()
     split_taps(w1_v, w1_hi, w1_lo, k1, 64)
@@ -455,7 +439,7 @@
     term_send[...] = jnp.where(upper, sent_terms[:, :128], sent_terms[:, 128:]).reshape(n_lat, MSG, 128)
     terms_sent = exchange(term_send, term_recv, t_send, t_recv)
 
-    rim_arrived(lat_ext, h_recv, h_send, (near_rows, corners, far_rows))
+    rim_arrived(lat_ext, h_recv, h_send, (edges, corners))
     for at, one, other in (
         (7, 1 - north, 2), (8, 9, 10 + south),
         (9, 2 * north, 1 - north), (10, 8, 9 + south),
@@ -526,7 +510,7 @@
                 g_ext[h, 2 + first_:2 + last, pl.ds(SIDE + parity, 32, stride=2), :] = (
                     grad2[held * parity:held * parity + held, 128 * h:128 * h + 128].reshape(last - first_, 32, 128))
         if dr:
-            rim2 += rim(g_ext, g_send, g_recv, (near_rows, far_rows), (dr,))
+            rim2 += rim(g_ext, g_send, g_recv, (edges,), (dr,))
             rim2 += packed_rim(corners, dr, g_send, g_recv)
         else:
             rim2 += packed_rim(sides, dr, g_send, g_recv)
@@ -582,29 +566,25 @@
     put2((((1, 4),), ((4, 7),), ((0, 3),)), ((0, 2, 6),))
     put_pairs(2, 8, 2)
     put3((((4, 8),), ((3, 7),), ((2, 6),)), ((2, 6),))
-    rim_arrived(g_ext, g_recv, g_send, (near_rows, far_rows), (1,))
+    rim_arrived(g_ext, g_recv, g_send, (edges,))
     packed_arrived(corners, 1, g_send, g_recv)
-    r10, r11 = pair_rows(g_ext, 10 + south), pair_rows(g_ext, 11 - south)
-    put_rows(sg_hi, sg_lo, 8, joined(pair_rows(g_ext, 9), r10))
-    put_rows(sg_hi, sg_lo, 10, joined(scaled_by(r10, 1.0 - southf), scaled_by(r11, 1.0 - southf)))
-    put_rows(sg_hi, sg_lo, 12, joined(plus(pair_rows(g_ext, 8), r10, southf), plus(pair_rows(g_ext, 9), r11, southf)))
-    put2((((10, 11),), ((8, 9),), ((12, 13),)), ((0, 8, 2),), True)
-    for m, (q7, q8, q9) in enumerate(zip(*[near_pairs(at, at + 1) for at in (7, 8, 9)])):
-        for at, piece in ((8, q8), (11, q9 * (1.0 - southf)), (13, q7 + southf * q9)):
-            sp_hi[m, at:at + 1], sp_lo[m, at:at + 1] = halves(piece)
-    put3((((8, 9), (11, 12)), ((7, 9),), ((6, 7), (13, 14))), ((6, 8),))
-
-    rim_arrived(g_ext, g_recv, g_send, (near_rows, far_rows), (-1,))
     packed_arrived(corners, -1, g_send, g_recv)
     r0, r1 = pair_rows(g_ext, north), pair_rows(g_ext, 1 - north)
+    r10, r11 = pair_rows(g_ext, 10 + south), pair_rows(g_ext, 11 - south)
     put_rows(sg_hi, sg_lo, 7, joined(r1, pair_rows(g_ext, 2)))
+    put_rows(sg_hi, sg_lo, 8, joined(pair_rows(g_ext, 9), r10))
     put_rows(sg_hi, sg_lo, 9, joined(plus(pair_rows(g_ext, 2), r0, northf), plus(pair_rows(g_ext, 3), r1, northf)))
+    put_rows(sg_hi, sg_lo, 10, joined(scaled_by(r10, 1.0 - southf), scaled_by(r11, 1.0 - southf)))
     put_rows(sg_hi, sg_lo, 11, joined(scaled_by(r0, 1.0 - northf), scaled_by(r1, 1.0 - northf)))
-    put2((((9, 10),), ((7, 8),), ((11, 12),)), ((0, 0, 2),), True)
-    for m, (q0, q1, q2) in enumerate(zip(*[near_pairs(at, at + 1) for at in (0, 1, 2)])):
-        for at, piece in ((1, q1), (10, q2 + northf * q0), (12, q0 * (1.0 - northf))):
+    put_rows(sg_hi, sg_lo, 12, joined(plus(pair_rows(g_ext, 8), r10, southf), plus(pair_rows(g_ext, 9), r11, southf)))
+    put2((((9, 11),), ((7, 9),), ((11, 13),)), ((0, 0, 2), (2, 8, 2)), True)
+
+    for m, (q0, q1, q2, q7, q8, q9) in enumerate(zip(*[near_pairs(at, at + 1) for at in (0, 1, 2, 7, 8, 9)])):
+        for at, piece in ((1, q1), (8, q8), (10, q2 + northf * q0), (11, q9 * (1.0 - southf)),
+                          (12, q0 * (1.0 - northf)), (13, q7 + southf * q9)):
             sp_hi[m, at:at + 1], sp_lo[m, at:at + 1] = halves(piece)
-    put3((((10, 11), (3, 4)), ((1, 3),), ((12, 13), (1, 2))), ((0, 2),))
+    put3((((10, 11), (3, 4), (8, 9), (11, 12)), ((1, 3), (7, 9)), ((12, 13), (1, 2), (6, 7), (13, 14))),
+         ((0, 2), (6, 8)))
     for copy in rim2:
         copy.wait_send()
 
@@ -647,8 +627,8 @@
         vmem((2, 10, PAIRS, hid), F32),
         vmem((4, 14, 32, hid), BF16), vmem((4, 14, 32, hid), BF16),
         pltpu.SemaphoreType.DMA((14,)),
-        pltpu.SemaphoreType.DMA((10,)), pltpu.SemaphoreType.DMA((11,)),
-        pltpu.SemaphoreType.DMA((10,)), pltpu.SemaphoreType.DMA((11,)),
+        pltpu.SemaphoreType.DMA((8,)), pltpu.SemaphoreType.DMA((9,)),
+        pltpu.SemaphoreType.DMA((8,)), pltpu.SemaphoreType.DMA((9,)),
     ] + [pltpu.SemaphoreType.DMA((1,))] * 4
     return pl.pallas_call(
         functools.partial(kernel, n_lon, n_lat, slots, patch, variables),

time: 38.3 us -> 34.9 us (0.911)
  Pallas kernels: 37.4 us -> 34.1 us
    pallas_call x1, Pallas kernels: 37.4 us -> 34.1 us  [shards(): pl.pallas_call(functools.partial(kernel, n_lon, n_lat, slots, patch, vari...]
where the time goes in v6:
time: 34.9 us; the launch traced here: 34.8 us
  Pallas kernels  34.1 us (98%)
  local copies, waits for them, and re-layouts  0.71 us (2%)
    pallas_call x1, Pallas kernels, shards(): pl.pallas_call(functools.partial(kernel, n_lon, n_lat, slots, patch, vari...  34.1 us
    unnamed x1, local copies, waits for them, and re-layouts  0.71 us

profile of v6, /device:TPU:1, one launch (start us, length us, event | category | flops | bytes accessed | tf_op | source)
XLA Modules:
  0.0 34.8 jit_solution(10443067667565294116)
XLA Ops:
  0.0 34.1 %shard_map.136 = f32[8,64,128]{2,1,0:T(8,128)S(1)} custom-call(f32[8,64,128]{2,1,0:T(8,128)} %latent.1, f32[1152,256]{1,0:T(8,128)} %bitcast.11, f32[1,256]{1,0:T(1,128)} %bitcast.13, f32[2304,256]{1,0:T(8,128)} %bitcast.9, f32[1,256]{1,0:T(1,128)} %bitcast.14, f32[4416,256]{1,0:T(8,128)} %bitcast.8, f32[4416]{0:T(1024)} %hbias.1, s32[64,512]{1,0:T(8,128)} %land.1, ...), custom_call_target="tpu_custom_call" | custom-call | tf_op jit(solution)/shard_map/pallas_call | solution.py:633
  34.1 0.7 %copy.16 = f32[8,64,128]{2,1,0:T(8,128)} copy(f32[8,64,128]{2,1,0:T(8,128)S(1)} %shard_map.136) | data formatting | bytes 524288

commit v7 on v6

--- a/solution.py
+++ b/solution.py
@@ -64,10 +64,10 @@
     k1 = latent.shape[2]
 
     loads = [
+        (land, land_v),
         (band, band_v.at[:, 0:n_lat * slots]),
         (cell, cell_v.at[:, 0:n_lat * slots]),
         (count, count_v.at[:, 0:n_lat * slots]),
-        (land, land_v),
         (latent, lat_ext.at[0, 2:10, SIDE:SIDE + 64, :]),
         (w1, w1_v),
         (b1, b1_v),
@@ -80,7 +80,7 @@
         (head, head_v),
     ]
     copies = [pltpu.make_async_copy(s, d, load_sem.at[i]) for i, (s, d) in enumerate(loads)]
-    (ld_band, ld_cell, ld_count, ld_land, ld_lat, ld_w1, ld_b1, ld_ok, ld_err, ld_hb, ld_w2, ld_b2, ld_value,
+    (ld_land, ld_band, ld_cell, ld_count, ld_lat, ld_w1, ld_b1, ld_ok, ld_err, ld_hb, ld_w2, ld_b2, ld_value,
      ld_head) = copies
     for copy in copies[:5]:
         copy.start()
@@ -278,7 +278,7 @@
 
     ld_band.wait()
     ld_cell.wait()
-    ld_count.wait()
+    ld_land.wait()
     lane = lax.broadcasted_iota(jnp.int32, (n_lat, 128), 1)
     live = lane < slots
 
@@ -286,7 +286,7 @@
         row = ref[...]
         return jnp.concatenate([row[:, slots * a:slots * a + 128] for a in range(n_lat)], axis=0)
 
-    bands, cells, counts = blocks(band_v), blocks(cell_v), blocks(count_v)
+    bands, cells = blocks(band_v), blocks(cell_v)
     below = (lax.broadcasted_iota(jnp.int32, (128, 128), 0) < lax.broadcasted_iota(jnp.int32, (128, 128), 1))
     below = below.astype(F32).astype(BF16)
     mine = jnp.where(live & (bands == lat), 1.0, 0.0)
@@ -296,7 +296,6 @@
     inner = (cell_row << 5) + (odd << 7) + (256 - 2 * 32)
     cells = pair + jnp.where((cell_row < 2) | (cell_row > 5), edge, inner)
     cellsf = cells.astype(F32) + 1.0
-    countsf = counts.astype(F32) * 0.125
     msg_k = lax.rem(lax.broadcasted_iota(jnp.int32, (MSG, 128), 0), CAP).astype(F32)
     land_k = lax.broadcasted_iota(jnp.int32, (LCAP, 128), 0).astype(F32)
     named = [jnp.sum(jnp.where(pick[a:a + 1] == land_k, cellsf[a:a + 1], 0.0), axis=1, keepdims=True)
@@ -305,7 +304,6 @@
     lrows = n_lat * LCAP
     messages = jnp.where(wanted == lax.broadcasted_iota(jnp.int32, (lrows, 512), 1), 1.0, 0.0).astype(BF16)
 
-    ld_land.wait()
     column = lax.broadcasted_iota(jnp.int32, (64, 512), 0)
     column = ((column & 31) << 1) + (column >> 5)
     fold = (lax.broadcasted_iota(jnp.int32, (64, 512), 1) >> 3) == column
@@ -325,11 +323,13 @@
     pl.semaphore_wait(barrier, len(around) + len(peers))
     land_sent = exchange(land_send, land_recv, l_send, l_recv)
     ld_lat.wait()
-    rim1 = rim(lat_ext, h_send, h_recv, (sides, edges, corners))
+    rim1 = rim(lat_ext, h_send, h_recv, (sides, corners, edges))
 
     ld_w1.wait()
     split_taps(w1_v, w1_hi, w1_lo, k1, 64)
 
+    ld_count.wait()
+    countsf = blocks(count_v).astype(F32) * 0.125
     first = lax.broadcasted_iota(jnp.int32, (MSG, 128), 0) < CAP
     taken = n_lat * CAP
     named, merged = [], []
@@ -499,21 +499,18 @@
     high, low = halves(came)
     came = jnp.concatenate([high, low], axis=1)
 
-    rim2 = []
-    for (first_, last, base), dr in zip(GROUPS, (-1, 1, 0)):
+    moved = nn(oht_msg[...], came)
+    grad2 = (hidden - moved[:, :hid] - moved[:, hid:]) * pre2[...]
+    for first_, last, base in GROUPS:
         held = 32 * (last - first_)
-        cells_ = slice(base, base + 2 * held)
-        moved = nn(oht_msg[cells_, :], came)
-        grad2 = (hidden[cells_] - moved[:, :hid] - moved[:, hid:]) * pre2[cells_, :]
         for parity in range(2):
+            at = base + held * parity
             for h in range(hid // 128):
                 g_ext[h, 2 + first_:2 + last, pl.ds(SIDE + parity, 32, stride=2), :] = (
-                    grad2[held * parity:held * parity + held, 128 * h:128 * h + 128].reshape(last - first_, 32, 128))
-        if dr:
-            rim2 += rim(g_ext, g_send, g_recv, (edges,), (dr,))
-            rim2 += packed_rim(corners, dr, g_send, g_recv)
-        else:
-            rim2 += packed_rim(sides, dr, g_send, g_recv)
+                    grad2[at:at + held, 128 * h:128 * h + 128].reshape(last - first_, 32, 128))
+    rim2 = packed_rim(sides, 0, g_send, g_recv)
+    rim2 += packed_rim(corners, -1, g_send, g_recv) + packed_rim(corners, 1, g_send, g_recv)
+    rim2 += rim(g_ext, g_send, g_recv, (edges,))
     terms_sent.wait_send()
 
     packed_arrived(sides, 0, g_send, g_recv)

time: 34.9 us -> 34.4 us (0.986); the launches traced: 34.8 us -> 33.8 us
  Pallas kernels: 34.1 us -> 33.1 us
    pallas_call x1, Pallas kernels: 34.1 us -> 33.1 us  [shards(): pl.pallas_call(functools.partial(kernel, n_lon, n_lat, slots, patch, vari...]
where the time goes in v7:
time: 34.4 us; the launch traced here: 33.8 us
  Pallas kernels  33.1 us (96%)
  local copies, waits for them, and re-layouts  0.71 us (2%)
    pallas_call x1, Pallas kernels, shards(): pl.pallas_call(functools.partial(kernel, n_lon, n_lat, slots, patch, vari...  33.1 us
    unnamed x1, local copies, waits for them, and re-layouts  0.71 us

profile of v7, /device:TPU:1, one launch (start us, length us, event | category | flops | bytes accessed | tf_op | source)
XLA Modules:
  0.0 33.8 jit_solution(5755442737302447705)
XLA Ops:
  0.0 33.1 %shard_map.136 = f32[8,64,128]{2,1,0:T(8,128)S(1)} custom-call(f32[8,64,128]{2,1,0:T(8,128)} %latent.1, f32[1152,256]{1,0:T(8,128)} %bitcast.11, f32[1,256]{1,0:T(1,128)} %bitcast.13, f32[2304,256]{1,0:T(8,128)} %bitcast.9, f32[1,256]{1,0:T(1,128)} %bitcast.14, f32[4416,256]{1,0:T(8,128)} %bitcast.8, f32[4416]{0:T(1024)} %hbias.1, s32[64,512]{1,0:T(8,128)} %land.1, ...), custom_call_target="tpu_custom_call" | custom-call | tf_op jit(solution)/shard_map/pallas_call | solution.py:630
  33.1 0.7 %copy.16 = f32[8,64,128]{2,1,0:T(8,128)} copy(f32[8,64,128]{2,1,0:T(8,128)S(1)} %shard_map.136) | data formatting | bytes 524288

commit v8 on v7

--- a/solution.py
+++ b/solution.py
@@ -376,7 +376,7 @@
         variable = place_ - pixel * variables
         chosen = lax.broadcasted_iota(jnp.int32, (variables, size), 0) == variable
         spread = nn(table, jnp.where(chosen, 1.0, 0.0).astype(BF16))
-        inv_row[:, at:at + size] = spread[0:1] + spread[1:2] + spread[2:3]
+        inv_row[:, at:at + size] = jnp.broadcast_to(spread[0:1] + spread[1:2] + spread[2:3], (8, size))
         which = lax.broadcasted_iota(jnp.int32, (128, size), 0)
         seen = jnp.where(which == pixel, spread[3:4], jnp.where(which == pixel + 64, spread[4:5], 0.0))
         ok_rows[:, at:at + size] = seen.astype(BF16)
@@ -385,7 +385,7 @@
     ld_value.wait()
     for at, size in spans:
         span = slice(at, at + size)
-        shifted = (value_v[:, span] - hb_v[span].reshape(1, size)) * inv_row[:, span]
+        shifted = (value_v[:, span] - hb_v[span].reshape(1, size)) * inv_row[0:1, span]
         val_hi[:, span], val_lo[:, span] = halves(shifted)
     ld_head.wait()
     split(head_v, head_hi, head_lo, 96)
@@ -473,7 +473,7 @@
         span = slice(at, at + size)
         both = nt(cols_both, head_hi[span, :])
         decoded = both[:taken] + both[taken:] + nt(cols_hi, head_lo[span, :])
-        high, low = halves(nn(flags_w[...], ok_rows[:, span]) * inv_row[:, span] * decoded)
+        high, low = halves(nn(flags_w[...], ok_rows[:, span]) * inv_row[0:1, span] * decoded)
         terms = back(high, low, at, size, terms)
 
     wanted_row = jnp.transpose(jnp.broadcast_to(wanted.astype(F32), (taken, 128)))[0:1, :].astype(jnp.int32)
@@ -560,7 +560,7 @@
                 done += last - first_
 
     inner_rows(g_ext, sg_hi, sg_lo)
-    put2((((1, 4),), ((4, 7),), ((0, 3),)), ((0, 2, 6),))
+    put2((((1, 4),), ((4, 7),), ((0, 3),)), ((0, 2, 6),), True)
     put_pairs(2, 8, 2)
     put3((((4, 8),), ((3, 7),), ((2, 6),)), ((2, 6),))
     rim_arrived(g_ext, g_recv, g_send, (edges,))
@@ -610,7 +610,7 @@
         vmem((1, padded), jnp.int32), vmem((1, padded), jnp.int32), vmem((1, padded), jnp.int32),
         vmem((slots, patch), F32), vmem((slots, patch), BF16), vmem((slots, patch), BF16),
         vmem((2 * slots, patch), BF16),
-        vmem((128, patch), BF16), vmem((1, patch), F32),
+        vmem((128, patch), BF16), vmem((8, patch), F32),
         vmem((512, 128), BF16), vmem((n_lat * CAP, 128), BF16),
         vmem((n_lat * CAP, 512), BF16), vmem((512, n_lat * CAP), BF16), vmem((512, rows), BF16),
         vmem((rows, 128), BF16),

time: 34.4 us -> 34.4 us (level)
  no operation moved by 1% of the time
where the time goes in v8:
time: 34.4 us; the launch traced here: 33.8 us
  Pallas kernels  33 us (96%)
  local copies, waits for them, and re-layouts  0.71 us (2%)
    pallas_call x1, Pallas kernels, shards(): pl.pallas_call(functools.partial(kernel, n_lon, n_lat, slots, patch, vari...  33 us
    unnamed x1, local copies, waits for them, and re-layouts  0.71 us

profile of v8, /device:TPU:1, one launch (start us, length us, event | category | flops | bytes accessed | tf_op | source)
XLA Modules:
  0.0 33.8 jit_solution(7843542037005617353)
XLA Ops:
  0.0 33.0 %shard_map.136 = f32[8,64,128]{2,1,0:T(8,128)S(1)} custom-call(f32[8,64,128]{2,1,0:T(8,128)} %latent.1, f32[1152,256]{1,0:T(8,128)} %bitcast.11, f32[1,256]{1,0:T(1,128)} %bitcast.13, f32[2304,256]{1,0:T(8,128)} %bitcast.9, f32[1,256]{1,0:T(1,128)} %bitcast.14, f32[4416,256]{1,0:T(8,128)} %bitcast.8, f32[4416]{0:T(1024)} %hbias.1, s32[64,512]{1,0:T(8,128)} %land.1, ...), custom_call_target="tpu_custom_call" | custom-call | tf_op jit(solution)/shard_map/pallas_call | solution.py:630
  33.1 0.7 %copy.16 = f32[8,64,128]{2,1,0:T(8,128)} copy(f32[8,64,128]{2,1,0:T(8,128)S(1)} %shard_map.136) | data formatting | bytes 524288
